TPU v7x, 512 devices: a whole 4x4x16 slice. The times are simulated.
512 devices in a mesh: fsdp: 64 (over z_lo, x, core), tp: 8 (over z_hi, y).
Axes of the slice: x: 4, y: 4, z: 16 (z_hi: 2, z_lo: 8; z = z_hi * 8 + z_lo), core: 2. Of those that a mesh axis runs over, the one named last changes fastest.
Arguments:
- train_inputs: bfloat16 [65536, 8192], P('fsdp', 'tp'), may hold values from -6 to 6
- key_cotangent: bfloat16 [65536, 1024], P('fsdp'), may hold values from -0.0234375 to 0.0234375
- master: float32 [8, 1024, 1024], P('tp', 'fsdp'), may hold values from -0.125 to 0.125
- moment_one: float32 [8, 1024, 1024], P('tp', 'fsdp'), may hold values from -6 to 6
- moment_two: float32 [8, 1024, 1024], P('tp', 'fsdp'), may hold values from 0.25 to 4
- step_inputs: bfloat16 [3, 256, 8192], P(None, 'fsdp', 'tp'), may hold values from -6 to 6
- decode_queries: bfloat16 [3, 256, 64, 128], P(None, 'fsdp', 'tp'), may hold values from -8 to 8
- step_values: bfloat16 [3, 256, 8, 128], P(None, 'fsdp', 'tp'), may hold values from -6 to 6
- cache_keys: bfloat16 [256, 8, 512, 128], P('fsdp', 'tp'), may hold values from -6 to 6
- cache_values: bfloat16 [256, 8, 512, 128], P('fsdp', 'tp'), may hold values from -6 to 6
- cache_lengths: int32 [256], P('fsdp'), may hold values from 128 to 512, as said below
- norm_gain: float32 [8192], replicated, may hold values from 0.1 to 1.9
Outputs:
- new_master: float32 [8, 1024, 1024], P('tp', 'fsdp')
- new_moment_one: float32 [8, 1024, 1024], P('tp', 'fsdp')
- new_moment_two: float32 [8, 1024, 1024], P('tp', 'fsdp')
- new_keys: bfloat16 [3, 256, 8, 128], P(None, 'fsdp', 'tp')
- decoded: bfloat16 [3, 256, 8192], P(None, 'fsdp', 'tp')
Inputs may be any that keep to these rules, and one draw needn't show every extreme that they name: `cache_lengths`: some row has exactly 512 live slots in every draw.
All inputs are finite; a program needn't handle non-finite values.
Results may differ from a plain program's by a relative error of at most 0.0055.
The roundings to bfloat16 on the way count: a program that leaves them out, or rounds other values in their place, can miss the bound.
Values may be sent and summed in bfloat16 or wider, within the bound.
A program may use at most 64 MiB of HBM per device.

v0:
```python
import jax
import jax.numpy as jnp
from jax import lax
from jax.sharding import PartitionSpec as P

correction_one = 1.0 - 0.9**4
correction_two = 1.0 - 0.95**4


def body(
    train_inputs,
    key_cotangent,
    master,
    moment_one,
    moment_two,
    step_inputs,
    decode_queries,
    step_values,
    cache_keys,
    cache_values,
    cache_lengths,
    norm_gain,
):
    contract_rows = (((0,), (0,)), ((), ()))
    owned_rows = master.shape[1]
    full_term = lax.dot_general(
        train_inputs, key_cotangent, contract_rows, preferred_element_type=jnp.float32
    )
    summed = lax.psum(full_term, "fsdp")
    gradient = lax.dynamic_slice_in_dim(
        summed, lax.axis_index("fsdp") * owned_rows, owned_rows, 0
    ).reshape(master.shape)
    new_moment_one = 0.9 * moment_one + 0.1 * gradient
    new_moment_two = 0.95 * moment_two + 0.05 * gradient * gradient
    new_master = master - 0.003 * (new_moment_one / correction_one) / (
        jnp.sqrt(new_moment_two / correction_two) + 1e-08
    )
    weights = new_master.reshape(master.shape[1], master.shape[2]).astype(jnp.bfloat16)
    steps_count = step_inputs.shape[0]
    rows = step_inputs.shape[1]
    kv_local = cache_keys.shape[1]
    slots = cache_keys.shape[2]
    head_size = cache_keys.shape[3]
    group = decode_queries.shape[2] // kv_local
    flat_rows = steps_count * rows
    whole_rows = lax.all_gather(step_inputs, "tp", axis=2, tiled=True)
    width = whole_rows.shape[2]
    inputs_flat = whole_rows.reshape(flat_rows, width).astype(jnp.float32)
    inverse = lax.rsqrt(jnp.mean(inputs_flat * inputs_flat, axis=-1, keepdims=True) + 1e-06)
    normed = (inputs_flat * inverse * norm_gain).astype(jnp.bfloat16)
    block_rows = lax.all_gather(weights, "fsdp", axis=0, tiled=True)
    head_cols = lax.all_to_all(block_rows, "tp", split_axis=1, concat_axis=0, tiled=True)
    key_sums = jnp.dot(normed, head_cols, preferred_element_type=jnp.float32)
    keys_flat = key_sums.astype(jnp.bfloat16)
    new_keys = keys_flat.reshape(steps_count, rows, kv_local, head_size)
    queries = decode_queries.reshape(steps_count, rows, kv_local, group, head_size)
    scale = 1.0 / head_size**0.5
    old_scores = (
        jnp.einsum("srkgd,rkpd->srkgp", queries, cache_keys, preferred_element_type=jnp.float32)
        * scale
    )
    slot_index = lax.broadcasted_iota(jnp.int32, (1, rows, 1, 1, slots), 4)
    live = slot_index < cache_lengths.reshape(1, rows, 1, 1, 1)
    old_scores = jnp.where(live, old_scores, -jnp.inf)
    new_scores = (
        jnp.einsum("srkgd,jrkd->srkgj", queries, new_keys, preferred_element_type=jnp.float32)
        * scale
    )
    step_index = lax.broadcasted_iota(jnp.int32, (steps_count, 1, 1, 1, steps_count), 0)
    key_index = lax.broadcasted_iota(jnp.int32, (steps_count, 1, 1, 1, steps_count), 4)
    new_scores = jnp.where(key_index <= step_index, new_scores, -jnp.inf)
    top = jnp.maximum(jnp.max(old_scores, axis=-1), jnp.max(new_scores, axis=-1))[..., None]
    old_weights = jnp.exp(old_scores - top)
    new_weights = jnp.exp(new_scores - top)
    total = jnp.sum(old_weights, axis=-1, keepdims=True) + jnp.sum(
        new_weights, axis=-1, keepdims=True
    )
    old_probs = (old_weights / total).astype(jnp.bfloat16)
    new_probs = (new_weights / total).astype(jnp.bfloat16)
    attended = jnp.einsum(
        "srkgp,rkpd->srkgd", old_probs, cache_values, preferred_element_type=jnp.float32
    )
    attended = attended + jnp.einsum(
        "srkgj,jrkd->srkgd", new_probs, step_values, preferred_element_type=jnp.float32
    )
    attended = attended.reshape(step_inputs.shape)
    decoded = (step_inputs.astype(jnp.float32) + attended).astype(jnp.bfloat16)
    return (new_master, new_moment_one, new_moment_two, new_keys, decoded)


def solution(mesh):
    return jax.shard_map(
        body,
        mesh=mesh,
        in_specs=(
            P("fsdp", "tp"),
            P("fsdp", None),
            P("tp", "fsdp", None),
            P("tp", "fsdp", None),
            P("tp", "fsdp", None),
            P(None, "fsdp", "tp"),
            P(None, "fsdp", "tp", None),
            P(None, "fsdp", "tp", None),
            P("fsdp", "tp", None, None),
            P("fsdp", "tp", None, None),
            P("fsdp"),
            P(),
        ),
        out_specs=(
            P("tp", "fsdp", None),
            P("tp", "fsdp", None),
            P("tp", "fsdp", None),
            P(None, "fsdp", "tp", None),
            P(None, "fsdp", "tp"),
        ),
        check_vma=False,
    )
```

profile of v0, /device:TPU:96, one launch (start us, length us, event | category | flops | bytes accessed | tf_op | source)
XLA Modules:
  0.0 1165.1 jit_solution(3800461744210858131)
XLA Ops:
  7.2 0.0 all-reduce.2.cloned.1.call-start
  7.2 1.5 copy-done
  8.8 5.9 fusion.28
  14.7 0.0 all-gather.3.cloned.1.call-start
  14.8 748.9 %all-reduce.2.cloned.1.call-done = f32[1024,1024]{1,0:T(8,128)} async-done(((f32[1024,1024]{1,0:T(8,128)}), f32[1024,1024]{1,0:T(8,128)}) %all-reduce.2.cloned.1.call-update) | async-done | bytes 4194320 | tf_op jit(solution)/shard_map/psum | solution.py:29
  763.7 1.5 fusion.24
  765.2 0.0 all-gather.3.cloned.1.call-update
  765.3 213.2 %all-gather.3.cloned.1.call-done = bf16[1,1024,1024]{2,1,0:T(8,128)(2,1)} async-done(((bf16[1,16,1024]{2,1,0:T(8,128)(2,1)}), bf16[1,1024,1024]{2,1,0:T(8,128)(2,1)}) %all-gather.3.cloned.1.call-update) | async-done | bytes 2097168 | tf_op jit(solution)/shard_map/all_gather | solution.py:51
  978.5 2.2 copy.38
  980.7 1.7 copy.23
  982.4 9.9 all-to-all-start
  992.2 159.8 %all_gather.6 = bf16[3,4,8192]{2,1,0:T(4,128)(2,1)S(1)} all-gather(bf16[3,4,1024]{2,1,0:T(4,128)(2,1)S(1)} %copy-done.2), channel_id=1, replica_groups=mesh['fsdp'=64,'tp'=8] {'tp'}, dimensions={2}, use_global_device_ids=true | all-gather | bytes 221184 | tf_op jit(solution)/shard_map/all_gather | solution.py:46
  1152.1 0.2 fusion.9
  1152.3 0.2 fusion.11
  1152.5 0.1 convert_element_type.34
  1152.5 0.1 iota_compare_fusion
  1152.6 0.3 fusion.26
  1153.0 2.0 convolution_convert_fusion
  1155.0 0.6 reshape.145
  1155.6 0.2 fusion.27
  1155.8 0.2 fusion.12
  1156.1 1.3 fusion.6
  1157.4 0.2 fusion.3
  1157.6 0.6 add_convert_fusion
  (29 shorter events, 0.2 us)
Async XLA Ops:
  7.2 1.6 copy-start
  7.2 756.5 %all-reduce.2.cloned.1.call-start = ((), (), s32[]{:S(2)}) async-start(), calls=%async_computation.1 | async-start | bytes 8388608 | tf_op jit(solution)/shard_map/psum | solution.py:29
  14.7 749.0 %copy-start.3 = (f32[1,16,1024]{2,1,0:T(8,128)S(1)}, f32[1,16,1024]{2,1,0:T(8,128)}, u32[]{:S(2)}) copy-start(f32[1,16,1024]{2,1,0:T(8,128)} %param.14) | copy-start | bytes 196612
  14.7 749.0 %copy-start.4 = (f32[1,16,1024]{2,1,0:T(8,128)S(1)}, f32[1,16,1024]{2,1,0:T(8,128)}, u32[]{:S(2)}) copy-start(f32[1,16,1024]{2,1,0:T(8,128)} %param.15) | copy-start | bytes 196612
  14.7 749.0 %copy-start.5 = (f32[1,16,1024]{2,1,0:T(8,128)S(1)}, f32[1,16,1024]{2,1,0:T(8,128)}, u32[]{:S(2)}) copy-start(f32[1,16,1024]{2,1,0:T(8,128)} %param.16) | copy-start | bytes 196612
  14.7 963.7 %all-gather.3.cloned.1.call-start = ((), (), s32[]{:S(2)}) async-start(), calls=%async_computation.2 | async-start | bytes 2129920 | tf_op jit(solution)/shard_map/all_gather | solution.py:51
  982.4 9.9 copy-start.2
  982.4 169.9 %copy-start.6 = (f32[8192]{0:T(1024)S(1)}, f32[8192]{0:T(1024)}, u32[]{:S(2)}) copy-start(f32[8192]{0:T(1024)} %param.23) | copy-start | bytes 98308
  982.4 170.2 %copy-start.8 = (s32[4]{0:T(128)S(1)}, s32[4]{0:T(128)}, u32[]{:S(2)}) copy-start(s32[4]{0:T(128)} %param.22) | copy-start | bytes 52
  982.4 170.3 %copy-start.1 = (bf16[4,1,512,128]{3,2,1,0:T(8,128)(2,1)S(1)}, bf16[4,1,512,128]{3,2,1,0:T(8,128)(2,1)}, u32[]{:S(2)}) copy-start(bf16[4,1,512,128]{3,2,1,0:T(8,128)(2,1)} %param.20) | copy-start | bytes 1572868
  982.4 170.3 %copy-start.7 = (bf16[3,4,8,128]{3,2,1,0:T(8,128)(2,1)S(1)}, bf16[3,4,8,128]{3,2,1,0:T(8,128)(2,1)}, u32[]{:S(2)}) copy-start(bf16[3,4,8,128]{3,2,1,0:T(8,128)(2,1)} %param.18) | copy-start | bytes 73732
  982.4 170.6 %all-to-all-start = ((bf16[1024,8,128]{2,0,1:T(8,128)(2,1)}), bf16[1024,8,128]{2,0,1:T(8,128)(2,1)}, u32[]{:S(2)}, u32[]{:S(2)}) async-start(bf16[1024,8,128]{2,0,1:T(8,128)(2,1)} %copy.23), calls=%async_computation | async-start | bytes 4194304 | tf_op jit(solution)/shard_map/all_to_all | solution.py:52
  1153.0 4.4 copy-start.9
Sparse Core Ops, SparseCore 0:
  14.9 748.7 all-reduce.1
  766.1 212.3 all-gather.2
where the time goes:
time: 1170 us
  waiting for transfers between devices  962 us (82%)
  blocking collectives  160 us (14%)
  between operations  14.2 us (1%)
    psum x1, waiting for transfers between devices, body(): summed = lax.psum(full_term, 'fsdp')  749 us
    all_gather x1, waiting for transfers between devices, body(): block_rows = lax.all_gather(weights, 'fsdp', axis=0, tiled=True)  213 us
    all_gather x1, blocking collectives, body(): whole_rows = lax.all_gather(step_inputs, 'tp', axis=2, tiled=True)  160 us
  transfers between devices with their start and end apart: 3, of which 2 were waited for; matrix products, arithmetic and copies ran while one was open for 0% of the time, Pallas kernels for 0%

commit v1 on v0

v1 whole, which is shorter than its diff:
```python
import functools

import jax
import jax.numpy as jnp
from jax import lax
from jax.experimental import pallas as pl
from jax.experimental.pallas import tpu as pltpu
from jax.sharding import PartitionSpec as P

MESH = pl.DeviceIdType.MESH
correction_one = 1.0 - 0.9**4
correction_two = 1.0 - 0.95**4

CHUNKS = 4
CW = 1024 // CHUNKS
F32 = jnp.float32
BF16 = jnp.bfloat16


class Copies:
    def __init__(self, send_sems, recv_sems):
        self.send_sems, self.recv_sems = send_sems, recv_sems
        self.made = []

    def send(self, src, dst, device):
        number = len(self.made)
        copy = pltpu.make_async_remote_copy(
            src_ref=src,
            dst_ref=dst,
            send_sem=self.send_sems.at[number],
            recv_sem=self.recv_sems.at[number],
            device_id=device,
            device_id_type=MESH,
        )
        copy.start()
        self.made.append(copy)
        return copy


N_COPIES = 25 + 11 * CHUNKS + 25


def kernel(
    x_hbm,
    c_hbm,
    master_hbm,
    one_hbm,
    two_hbm,
    step_hbm,
    query_hbm,
    value_hbm,
    ck_hbm,
    cv_hbm,
    lengths,
    gain_hbm,
    new_master,
    new_one,
    new_two,
    keys_out,
    att_out,
    x_v,
    c_v,
    adam_v,
    step_v,
    query_v,
    value_v,
    ck_v,
    cv_v,
    gain_v,
    part,
    part_in,
    ring_out,
    ring_in,
    line_sum,
    pair_out,
    pair_in,
    quad_sum,
    quad_out,
    quad_in,
    rows32,
    rows_y,
    rows_z,
    squares,
    normed,
    w_out,
    w_all,
    key_part,
    key_in,
    q32,
    old_exp,
    old_top,
    old_sum,
    sv32,
    local_sems,
    send_sems,
    recv_sems,
):
    f, t = lax.axis_index("fsdp"), lax.axis_index("tp")
    core = lax.rem(f, 2)
    x = lax.rem(lax.div(f, 2), 4)
    zl = lax.div(f, 8)
    y = lax.rem(t, 4)
    zh = lax.div(t, 4)
    z = zh * 8 + zl

    def fsdp(zl_, x_, core_):
        return (zl_ * 4 + x_) * 2 + core_

    def at(zl_=zl, x_=x, core_=core, zh_=zh, y_=y):
        return {"fsdp": fsdp(zl_, x_, core_), "tp": zh_ * 4 + y_}

    sibling = at(core_=1 - core)
    x_peer = [None] + [at(x_=lax.rem(x + k, 4)) for k in (1, 2, 3)]
    y_peer = [None] + [at(y_=lax.rem(y + k, 4)) for k in (1, 2, 3)]

    def z_of(k):
        return lax.rem(z + k, 16)

    def z_peer(k):
        other = z_of(k)
        return at(zl_=lax.rem(other, 8), zh_=lax.div(other, 8))

    barrier = pltpu.get_barrier_semaphore()
    partners = [sibling] + x_peer[1:] + y_peer[1:] + [z_peer(k) for k in range(1, 16)]
    for partner in partners:
        pl.semaphore_signal(barrier, inc=1, device_id=partner, device_id_type=MESH)

    loads = []
    for number, (src, dst) in enumerate(
        (
            (x_hbm, x_v),
            (c_hbm, c_v),
            (step_hbm, step_v),
            (query_hbm, query_v),
            (ck_hbm, ck_v),
            (cv_hbm, cv_v),
            (value_hbm, value_v),
            (gain_hbm, gain_v),
            (master_hbm, adam_v.at[0]),
            (one_hbm, adam_v.at[1]),
            (two_hbm, adam_v.at[2]),
        )
    ):
        load = pltpu.make_async_copy(src, dst, local_sems.at[number])
        load.start()
        loads.append(load)

    loads[2].wait()
    rows32[...] = jnp.zeros_like(rows32)
    for s in range(3):
        rows32[4 * s : 4 * s + 4, :] = step_v[s].astype(F32)
    for k in range(8):
        rows_y[y, k] = rows32[:, 128 * k : 128 * k + 128].astype(BF16)

    loads[0].wait()
    loads[1].wait()
    for j in range(CHUNKS):

        @pl.loop(0, 8)
        def _(m):
            columns = pl.ds(pl.multiple_of(m * 128, 128), 128)
            term = lax.dot_general(
                x_v[:, columns],
                c_v[:, j * CW : (j + 1) * CW],
                (((0,), (0,)), ((), ())),
                preferred_element_type=F32,
            ).reshape(4, 2, 16, CW)
            part[j, 0, m] = term[:, 0]
            part[j, 1, m] = term[:, 1]

    pl.semaphore_wait(barrier, len(partners))
    copies = Copies(send_sems, recv_sems)

    own_rows = [copies.send(rows_y.at[y], rows_y.at[y], y_peer[k]) for k in (1, 2, 3)]
    swaps = [
        copies.send(part.at[j, 1 - core], part_in.at[j], sibling) for j in range(CHUNKS)
    ]

    xp, xo, xm = (lax.rem(x + k, 4) for k in (1, 2, 3))
    low, high = slice(0, 4), slice(4, 8)
    ring, pairs, quads = {}, {}, {}
    parity, quad = lax.rem(zl, 2), lax.div(zl, 2)

    def chip_sum(j, half, target):
        return part[j, core, half, target] + part_in[j, half, target]

    def ring_send(j, number, value, device):
        ring_out[j, number] = value.astype(BF16)
        ring[j, number] = copies.send(ring_out.at[j, number], ring_in.at[j, number], device)

    def ring_first(j):
        swaps[j].wait_recv()
        ring_send(j, 0, chip_sum(j, low, xo), x_peer[1])
        ring_send(j, 1, chip_sum(j, high, xo), x_peer[3])
        ring_send(j, 2, chip_sum(j, high, xp), x_peer[1])
        ring_send(j, 3, chip_sum(j, low, xm), x_peer[3])

    def ring_second(j):
        ring[j, 0].wait_recv()
        ring_send(j, 4, chip_sum(j, low, xp) + ring_in[j, 0].astype(F32), x_peer[1])
        ring[j, 1].wait_recv()
        ring_send(j, 5, chip_sum(j, high, xm) + ring_in[j, 1].astype(F32), x_peer[3])

    def line_pair(j):
        for number in (2, 3, 4, 5):
            ring[j, number].wait_recv()
        line_sum[j, low] = (
            chip_sum(j, low, x) + ring_in[j, 3].astype(F32) + ring_in[j, 4].astype(F32)
        )
        line_sum[j, high] = (
            chip_sum(j, high, x) + ring_in[j, 2].astype(F32) + ring_in[j, 5].astype(F32)
        )
        for q in range(4):
            pair_out[j, q] = line_sum[j, 2 * q + 1 - parity].astype(BF16)
        pairs[j] = copies.send(
            pair_out.at[j], pair_in.at[j], at(zl_=zl + 1 - 2 * parity)
        )

    def line_quad(j):
        pairs[j].wait_recv()
        for q in range(4):
            total = line_sum[j, 2 * q + parity] + pair_in[j, q].astype(F32)
            quad_sum[j, q] = total
            quad_out[j, q] = total.astype(BF16)
        for k in (2, 3, 1):
            other = lax.rem(quad + k, 4)
            quads[j, k] = copies.send(
                quad_out.at[j, other], quad_in.at[j, k - 1], at(zl_=2 * other + parity)
            )

    def update(j):
        for k in (1, 2, 3):
            quads[j, k].wait_recv()
        gradient = quad_sum[j, quad]
        for k in (1, 2, 3):
            gradient = gradient + quad_in[j, k - 1].astype(F32)
        columns = slice(j * CW, (j + 1) * CW)
        one = 0.9 * adam_v[1, 0, :, columns] + 0.1 * gradient
        two = 0.95 * adam_v[2, 0, :, columns] + 0.05 * gradient * gradient
        fresh = adam_v[0, 0, :, columns] - 0.003 * (one / correction_one) / (
            jnp.sqrt(two / correction_two) + 1e-08
        )
        new_one[0, :, columns] = one
        new_two[0, :, columns] = two
        new_master[0, :, columns] = fresh
        weights = fresh.astype(BF16)
        for k in range(CW // 128):
            head = j * (CW // 128) + k
            w_out[head % 4, head // 4] = weights[:, 128 * k : 128 * k + 128]

    lane = lax.broadcasted_iota(jnp.int32, (16, 128), 1)
    diagonal = lane == lax.broadcasted_iota(jnp.int32, (16, 128), 0)
    spread, rows_sent = {}, {}

    def send_rows():
        for copy in own_rows:
            copy.wait_recv()
        for k in (4, 3, 5, 2, 6, 1, 7):
            other = lax.rem(zl + k, 8)
            rows_sent[k] = copies.send(rows_y.at[:, other], rows_z.at[zl], at(zl_=other))
        total = jnp.zeros((16, 128), F32)
        for q in range(4):
            for k in range(8):
                block = rows_y[q, k].astype(F32)
                total = total + block * block
        column = jnp.sum(total, axis=1, keepdims=True)
        squares[z] = jnp.sum(jnp.where(diagonal, column, 0.0), axis=0, keepdims=True)
        for k in (8, 7, 9, 6, 10, 5, 11, 4, 12, 3, 13, 2, 14, 1, 15):
            spread[k] = copies.send(squares.at[z], squares.at[z], z_peer(k))
        for q in range(4):
            rows_z[zl, q] = rows_y[q, zl]

    def make_normed():
        for k in range(1, 16):
            spread[k].wait_recv()
        for k in range(1, 8):
            rows_sent[k].wait_recv()
        for s in range(8):
            both = squares[s] + squares[s + 8]
            column = jnp.sum(jnp.where(diagonal, both, 0.0), axis=1, keepdims=True)
            inverse = lax.rsqrt(column * (1.0 / 8192.0) + 1e-06)
            for q in range(4):
                gain = gain_v[pl.ds((zh * 4 + q) * 8 + zl, 1), :]
                block = rows_z[s, q].astype(F32) * inverse * gain
                normed[16 * s : 16 * s + 16, 128 * q : 128 * q + 128] = block.astype(BF16)

    scale = 1.0 / 128.0**0.5

    def old_scores():
        for number in (3, 4, 5, 6):
            loads[number].wait()
        q32[...] = jnp.zeros_like(q32)
        for s in range(3):
            for r in range(4):
                q32[32 * r + 8 * s : 32 * r + 8 * s + 8, :] = query_v[s, r].astype(F32)
        sv32[...] = jnp.zeros_like(sv32)
        for s in range(3):
            sv32[4 * s : 4 * s + 4, :] = value_v[s, :, 0, :].astype(F32)
        slot = lax.broadcasted_iota(jnp.int32, (32, 512), 1)
        for r in range(4):
            scores = (
                lax.dot_general(
                    q32[32 * r : 32 * r + 32, :].astype(BF16),
                    ck_v[r, 0],
                    (((1,), (1,)), ((), ())),
                    preferred_element_type=F32,
                )
                * scale
            )
            scores = jnp.where(slot < lengths[r], scores, -jnp.inf)
            top = jnp.max(scores, axis=1, keepdims=True)
            weight = jnp.exp(scores - top)
            rows = slice(32 * r, 32 * r + 32)
            old_exp[rows, :] = weight
            old_top[rows, :] = top
            old_sum[rows, :] = jnp.sum(weight, axis=1, keepdims=True)

    ring_first(0)
    send_rows()
    ring_first(1)
    ring_second(0)
    line_pair(0)
    ring_first(2)
    ring_second(1)
    old_scores()
    line_quad(0)
    line_pair(1)
    ring_first(3)
    ring_second(2)
    line_quad(1)
    line_pair(2)
    ring_second(3)
    for number in range(7, 11):
        loads[number].wait()
    update(0)
    line_quad(2)
    line_pair(3)
    make_normed()
    update(1)
    line_quad(3)
    update(2)
    update(3)

    to_y = []
    for k in (2, 1, 3):
        other = lax.rem(y + k, 4)
        to_y.append(copies.send(w_out.at[other], w_all.at[:, y, x, core], y_peer[k]))
    for h in range(2):
        w_all[h, y, x, core] = w_out[y, h]
    for copy in to_y:
        copy.wait_recv()
    mine = w_all.at[:, :, x, core]
    to_x = [(k, copies.send(mine, mine, x_peer[k])) for k in (2, 1, 3)]
    to_core = [copies.send(mine, mine, sibling)]
    for k, copy in (to_x[1], to_x[2], to_x[0]):
        copy.wait_recv()
        theirs = w_all.at[:, :, lax.rem(x + 4 - k, 4), core]
        to_core.append(copies.send(theirs, theirs, sibling))
    for copy in to_core:
        copy.wait_recv()

    for h in range(2):
        key_part[h] = jnp.dot(
            normed[...], w_all[h].reshape(512, 128), preferred_element_type=F32
        ).reshape(8, 16, 128)
    to_z = []
    for k in (8, 7, 9, 6, 10, 5, 11, 4, 12, 3, 13, 2, 14, 1, 15):
        other = z_of(k)
        to_z.append(
            copies.send(
                key_part.at[lax.div(other, 8), lax.rem(other, 8)], key_in.at[z], z_peer(k)
            )
        )
    key_in[z] = key_part[zh, zl]
    for copy in to_z:
        copy.wait_recv()
    keys = key_in[0]
    for k in range(1, 16):
        keys = keys + key_in[k]
    keys = keys.astype(BF16)
    keys_out[...] = keys.astype(F32)

    new = (
        lax.dot_general(
            q32[...].astype(BF16), keys, (((1,), (1,)), ((), ())), preferred_element_type=F32
        )
        * scale
    )
    row = lax.broadcasted_iota(jnp.int32, (128, 16), 0)
    column = lax.broadcasted_iota(jnp.int32, (128, 16), 1)
    same_row = (row // 32) == (column % 4)
    earlier = (column // 4) <= ((row % 32) // 8)
    new = jnp.where(same_row & earlier & (column < 12), new, -jnp.inf)
    top = jnp.maximum(old_top[...], jnp.max(new, axis=1, keepdims=True))
    fade = jnp.exp(old_top[...] - top)
    new = jnp.exp(new - top)
    total = old_sum[...] * fade + jnp.sum(new, axis=1, keepdims=True)
    new_probs = (new / total).astype(BF16)
    share = fade / total
    attended = jnp.dot(new_probs, sv32[...].astype(BF16), preferred_element_type=F32)
    for r in range(4):
        rows = slice(32 * r, 32 * r + 32)
        probs = (old_exp[rows, :] * share[rows]).astype(BF16)
        att = attended[rows] + jnp.dot(probs, cv_v[r, 0], preferred_element_type=F32)
        for s in range(3):
            att_out[s, r] = att[8 * s : 8 * s + 8]

    for copy in copies.made:
        copy.wait_send()
    assert len(copies.made) == N_COPIES, len(copies.made)


def body(
    train_inputs,
    key_cotangent,
    master,
    moment_one,
    moment_two,
    step_inputs,
    decode_queries,
    step_values,
    cache_keys,
    cache_values,
    cache_lengths,
    norm_gain,
):
    anywhere = pl.BlockSpec(memory_space=pl.ANY)
    vmem = pl.BlockSpec(memory_space=pltpu.VMEM)
    owned = jax.ShapeDtypeStruct(master.shape, F32)
    new_master, new_one, new_two, keys, attended = pl.pallas_call(
        kernel,
        out_shape=(
            owned,
            owned,
            owned,
            jax.ShapeDtypeStruct((16, 128), F32),
            jax.ShapeDtypeStruct((3, 4, 8, 128), F32),
        ),
        in_specs=[anywhere] * 10 + [pl.BlockSpec(memory_space=pltpu.SMEM), anywhere],
        out_specs=(vmem,) * 5,
        scratch_shapes=[
            pltpu.VMEM((1024, 1024), BF16),
            pltpu.VMEM((1024, 1024), BF16),
            pltpu.VMEM((3, 1, 16, 1024), F32),
            pltpu.VMEM((3, 4, 1024), BF16),
            pltpu.VMEM((3, 4, 8, 128), BF16),
            pltpu.VMEM((3, 4, 1, 128), BF16),
            pltpu.VMEM((4, 1, 512, 128), BF16),
            pltpu.VMEM((4, 1, 512, 128), BF16),
            pltpu.VMEM((64, 128), F32),
            pltpu.VMEM((CHUNKS, 2, 8, 4, 16, CW), F32),
            pltpu.VMEM((CHUNKS, 8, 4, 16, CW), F32),
            pltpu.VMEM((CHUNKS, 6, 4, 16, CW), BF16),
            pltpu.VMEM((CHUNKS, 6, 4, 16, CW), BF16),
            pltpu.VMEM((CHUNKS, 8, 16, CW), F32),
            pltpu.VMEM((CHUNKS, 4, 16, CW), BF16),
            pltpu.VMEM((CHUNKS, 4, 16, CW), BF16),
            pltpu.VMEM((CHUNKS, 4, 16, CW), F32),
            pltpu.VMEM((CHUNKS, 4, 16, CW), BF16),
            pltpu.VMEM((CHUNKS, 3, 16, CW), BF16),
            pltpu.VMEM((16, 1024), F32),
            pltpu.VMEM((4, 8, 16, 128), BF16),
            pltpu.VMEM((8, 4, 16, 128), BF16),
            pltpu.VMEM((16, 1, 128), F32),
            pltpu.VMEM((128, 512), BF16),
            pltpu.VMEM((4, 2, 16, 128), BF16),
            pltpu.VMEM((2, 4, 4, 2, 16, 128), BF16),
            pltpu.VMEM((2, 8, 16, 128), F32),
            pltpu.VMEM((16, 16, 128), F32),
            pltpu.VMEM((128, 128), F32),
            pltpu.VMEM((128, 512), F32),
            pltpu.VMEM((128, 1), F32),
            pltpu.VMEM((128, 1), F32),
            pltpu.VMEM((16, 128), F32),
            pltpu.SemaphoreType.DMA((11,)),
            pltpu.SemaphoreType.DMA((N_COPIES,)),
            pltpu.SemaphoreType.DMA((N_COPIES,)),
        ],
        compiler_params=pltpu.CompilerParams(
            collective_id=0, has_side_effects=True, vmem_limit_bytes=48 << 20
        ),
        name="adam_decode",
    )(
        train_inputs,
        key_cotangent,
        master,
        moment_one,
        moment_two,
        step_inputs,
        decode_queries,
        step_values,
        cache_keys,
        cache_values,
        cache_lengths,
        norm_gain.reshape(64, 128),
    )
    new_keys = keys[:12].reshape(step_values.shape).astype(BF16)
    decoded = (step_inputs.astype(F32) + attended.reshape(step_inputs.shape)).astype(BF16)
    return new_master, new_one, new_two, new_keys, decoded


def solution(mesh):
    return jax.shard_map(
        body,
        mesh=mesh,
        in_specs=(
            P("fsdp", "tp"),
            P("fsdp", None),
            P("tp", "fsdp", None),
            P("tp", "fsdp", None),
            P("tp", "fsdp", None),
            P(None, "fsdp", "tp"),
            P(None, "fsdp", "tp", None),
            P(None, "fsdp", "tp", None),
            P("fsdp", "tp", None, None),
            P("fsdp", "tp", None, None),
            P("fsdp"),
            P(),
        ),
        out_specs=(
            P("tp", "fsdp", None),
            P("tp", "fsdp", None),
            P("tp", "fsdp", None),
            P(None, "fsdp", "tp", None),
            P(None, "fsdp", "tp"),
        ),
        check_vma=False,
    )
```

time: 1170 us -> 87.9 us (0.08)
  the two profiles are of different devices: /device:TPU:96 before, /device:TPU:1 now
where the time goes in v1:
time: 87.9 us; the launch traced here: 87.2 us
  Pallas kernels  72 us (82%)
  local copies, waits for them, and re-layouts  13.9 us (16%)
    pallas_call x1, Pallas kernels, body(): pl.pallas_call(kernel, out_shape=(owned, owned, owned, jax.ShapeDtypeStru...  72 us
    unnamed x28, local copies, waits for them, and re-layouts  13.2 us

profile of v1, /device:TPU:1, one launch (start us, length us, event | category | flops | bytes accessed | tf_op | source)
XLA Modules:
  0.0 87.2 jit_solution(18397890631442860252)
XLA Ops:
  0.6 0.7 copy.17.value_hbm
  1.3 0.0 copy-start
  1.3 1.6 %copy-done = bf16[1024,1024]{1,0:T(8,128)(2,1)S(1)} copy-done((bf16[1024,1024]{1,0:T(8,128)(2,1)S(1)}, bf16[1024,1024]{1,0:T(8,128)(2,1)}, u32[]{:S(2)}) %copy-start) | copy-done | bytes 2097176
  2.9 0.0 copy-start.1
  2.9 1.6 %copy-done.1 = bf16[1024,1024]{1,0:T(8,128)(2,1)S(1)} copy-done((bf16[1024,1024]{1,0:T(8,128)(2,1)S(1)}, bf16[1024,1024]{1,0:T(8,128)(2,1)}, u32[]{:S(2)}) %copy-start.1) | copy-done | bytes 2097176
  4.5 1.0 %copy-done.2 = bf16[4,1,512,128]{3,2,1,0:T(8,128)(2,1)S(1)} copy-done((bf16[4,1,512,128]{3,2,1,0:T(8,128)(2,1)S(1)}, bf16[4,1,512,128]{3,2,1,0:T(8,128)(2,1)}, u32[]{:S(2)}) %copy-start.2) | copy-done | bytes 524312
  5.5 0.0 copy-start.3
  5.5 1.0 %copy-done.3 = bf16[4,1,512,128]{3,2,1,0:T(8,128)(2,1)S(1)} copy-done((bf16[4,1,512,128]{3,2,1,0:T(8,128)(2,1)S(1)}, bf16[4,1,512,128]{3,2,1,0:T(8,128)(2,1)}, u32[]{:S(2)}) %copy-start.3) | copy-done | bytes 524312
  6.6 0.0 copy-start.4
  6.6 0.7 copy-done.4
  7.3 0.0 copy-start.6
  7.3 0.8 copy-done.6
  8.2 0.8 copy-done.7
  9.0 0.8 copy-done.8
  9.8 0.8 copy-done.9
  10.6 0.7 copy-done.10
  11.3 0.7 copy-done.11
  12.0 72.0 %adam_decode.1 = (f32[1,16,1024]{2,1,0:T(8,128)S(1)}, f32[1,16,1024]{2,1,0:T(8,128)S(1)}, f32[1,16,1024]{2,1,0:T(8,128)S(1)}, f32[16,128]{1,0:T(8,128)S(1)}, f32[3,4,8,128]{3,2,1,0:T(8,128)S(1)}) custom-call(bf16[1024,1024]{1,0:T(8,128)(2,1)S(1)} %copy-done, bf16[1024,1024]{1,0:T(8,128)(2,1)S(1)} %copy-done.1, f32[1,16,1024]{2,1,0:T(8,128)S(1)} %copy-done.6, ...), custom_call_target="tpu_custom_call" | custom-call | tf_op jit(solution)/shard_map/adam_decode/pallas_call | solution.py:430
  84.1 0.0 copy-done.5
  84.1 0.6 add_convert_fusion
  84.7 0.6 convert_element_type.18
  85.3 0.6 copy.22
  85.9 0.6 copy.23
  86.6 0.6 copy.24
  (9 shorter events, 0.0 us)
Async XLA Ops:
  1.3 1.6 %copy-start = (bf16[1024,1024]{1,0:T(8,128)(2,1)S(1)}, bf16[1024,1024]{1,0:T(8,128)(2,1)}, u32[]{:S(2)}) copy-start(bf16[1024,1024]{1,0:T(8,128)(2,1)} %x_hbm.1) | copy-start | bytes 6291460
  2.9 1.6 %copy-start.1 = (bf16[1024,1024]{1,0:T(8,128)(2,1)S(1)}, bf16[1024,1024]{1,0:T(8,128)(2,1)}, u32[]{:S(2)}) copy-start(bf16[1024,1024]{1,0:T(8,128)(2,1)} %c_hbm.1) | copy-start | bytes 6291460
  4.5 1.0 %copy-start.2 = (bf16[4,1,512,128]{3,2,1,0:T(8,128)(2,1)S(1)}, bf16[4,1,512,128]{3,2,1,0:T(8,128)(2,1)}, u32[]{:S(2)}) copy-start(bf16[4,1,512,128]{3,2,1,0:T(8,128)(2,1)} %ck_hbm.1) | copy-start | bytes 1572868
  5.5 1.0 %copy-start.3 = (bf16[4,1,512,128]{3,2,1,0:T(8,128)(2,1)S(1)}, bf16[4,1,512,128]{3,2,1,0:T(8,128)(2,1)}, u32[]{:S(2)}) copy-start(bf16[4,1,512,128]{3,2,1,0:T(8,128)(2,1)} %cv_hbm.1) | copy-start | bytes 1572868
  6.6 0.7 copy-start.4
  7.3 0.8 copy-start.6
  8.2 0.8 copy-start.7
  9.0 0.8 copy-start.8
  9.8 0.8 copy-start.9
  10.6 0.7 copy-start.10
  11.3 0.7 copy-start.11
  12.0 72.1 %copy-start.5 = (bf16[3,4,1024]{2,1,0:T(4,128)(2,1)S(1)}, bf16[3,4,1024]{2,1,0:T(4,128)(2,1)}, u32[]{:S(2)}) copy-start(bf16[3,4,1024]{2,1,0:T(4,128)(2,1)} %step_hbm.1) | copy-start | bytes 73732

commit v2 on v1

--- a/solution.py
+++ b/solution.py
@@ -22,13 +22,13 @@
         self.send_sems, self.recv_sems = send_sems, recv_sems
         self.made = []
 
-    def send(self, src, dst, device):
+    def send(self, src, dst, device, recv_sem=None):
         number = len(self.made)
         copy = pltpu.make_async_remote_copy(
             src_ref=src,
             dst_ref=dst,
             send_sem=self.send_sems.at[number],
-            recv_sem=self.recv_sems.at[number],
+            recv_sem=self.recv_sems.at[number] if recv_sem is None else recv_sem,
             device_id=device,
             device_id_type=MESH,
         )
@@ -37,7 +37,7 @@
         return copy
 
 
-N_COPIES = 25 + 11 * CHUNKS + 25
+N_COPIES = 25 + 11 * CHUNKS + 35
 
 
 def kernel(
@@ -94,6 +94,8 @@
     local_sems,
     send_sems,
     recv_sems,
+    key_sems,
+    far_sems,
 ):
     f, t = lax.axis_index("fsdp"), lax.axis_index("tp")
     core = lax.rem(f, 2)
@@ -121,7 +123,10 @@
         return at(zl_=lax.rem(other, 8), zh_=lax.div(other, 8))
 
     barrier = pltpu.get_barrier_semaphore()
-    partners = [sibling] + x_peer[1:] + y_peer[1:] + [z_peer(k) for k in range(1, 16)]
+    group = [sibling] + [
+        at(x_=lax.rem(x + k, 4), core_=c_) for k in (2, 1, 3) for c_ in (core, 1 - core)
+    ]
+    partners = group + y_peer[1:] + [z_peer(1), z_peer(15)]
     for partner in partners:
         pl.semaphore_signal(barrier, inc=1, device_id=partner, device_id_type=MESH)
 
@@ -152,29 +157,36 @@
     for k in range(8):
         rows_y[y, k] = rows32[:, 128 * k : 128 * k + 128].astype(BF16)
 
+    pl.semaphore_wait(barrier, len(partners))
+    copies = Copies(send_sems, recv_sems)
+
+    def hop(d):
+        if d > 0:
+            pl.semaphore_wait(far_sems.at[d - 1, 0], 1)
+            pl.semaphore_wait(far_sems.at[d - 1, 1], 1)
+        if d < 7:
+            for side, partner in enumerate((z_peer(1), z_peer(15))):
+                pl.semaphore_signal(
+                    far_sems.at[d, side], inc=1, device_id=partner, device_id_type=MESH
+                )
+
+    hop(0)
+    own_rows = [copies.send(rows_y.at[y], rows_y.at[y], y_peer[k]) for k in (2, 1, 3)]
+
     loads[0].wait()
     loads[1].wait()
+    swaps = []
     for j in range(CHUNKS):
-
-        @pl.loop(0, 8)
-        def _(m):
-            columns = pl.ds(pl.multiple_of(m * 128, 128), 128)
-            term = lax.dot_general(
-                x_v[:, columns],
-                c_v[:, j * CW : (j + 1) * CW],
-                (((0,), (0,)), ((), ())),
-                preferred_element_type=F32,
-            ).reshape(4, 2, 16, CW)
-            part[j, 0, m] = term[:, 0]
-            part[j, 1, m] = term[:, 1]
-
-    pl.semaphore_wait(barrier, len(partners))
-    copies = Copies(send_sems, recv_sems)
-
-    own_rows = [copies.send(rows_y.at[y], rows_y.at[y], y_peer[k]) for k in (1, 2, 3)]
-    swaps = [
-        copies.send(part.at[j, 1 - core], part_in.at[j], sibling) for j in range(CHUNKS)
-    ]
+        term = lax.dot_general(
+            x_v[...],
+            c_v[:, j * CW : (j + 1) * CW],
+            (((0,), (0,)), ((), ())),
+            preferred_element_type=F32,
+        ).reshape(8, 4, 2, 16, CW)
+        part[j, 0] = term[:, :, 0]
+        part[j, 1] = term[:, :, 1]
+        swaps.append(copies.send(part.at[j, 1 - core], part_in.at[j], sibling))
+        hop(j + 1)
 
     xp, xo, xm = (lax.rem(x + k, 4) for k in (1, 2, 3))
     low, high = slice(0, 4), slice(4, 8)
@@ -246,7 +258,7 @@
         weights = fresh.astype(BF16)
         for k in range(CW // 128):
             head = j * (CW // 128) + k
-            w_out[head % 4, head // 4] = weights[:, 128 * k : 128 * k + 128]
+            w_out[head // 4, head % 4] = weights[:, 128 * k : 128 * k + 128]
 
     lane = lax.broadcasted_iota(jnp.int32, (16, 128), 1)
     diagonal = lane == lax.broadcasted_iota(jnp.int32, (16, 128), 0)
@@ -295,7 +307,7 @@
                 q32[32 * r + 8 * s : 32 * r + 8 * s + 8, :] = query_v[s, r].astype(F32)
         sv32[...] = jnp.zeros_like(sv32)
         for s in range(3):
-            sv32[4 * s : 4 * s + 4, :] = value_v[s, :, 0, :].astype(F32)
+            sv32[4 * s : 4 * s + 4, :] = value_v[s].astype(F32)
         slot = lax.broadcasted_iota(jnp.int32, (32, 512), 1)
         for r in range(4):
             scores = (
@@ -315,99 +327,161 @@
             old_top[rows, :] = top
             old_sum[rows, :] = jnp.sum(weight, axis=1, keepdims=True)
 
-    ring_first(0)
-    send_rows()
-    ring_first(1)
-    ring_second(0)
-    line_pair(0)
-    ring_first(2)
-    ring_second(1)
-    old_scores()
-    line_quad(0)
-    line_pair(1)
-    ring_first(3)
-    ring_second(2)
-    line_quad(1)
-    line_pair(2)
-    ring_second(3)
-    for number in range(7, 11):
-        loads[number].wait()
-    update(0)
-    line_quad(2)
-    line_pair(3)
-    make_normed()
-    update(1)
-    line_quad(3)
-    update(2)
-    update(3)
-
-    to_y = []
-    for k in (2, 1, 3):
-        other = lax.rem(y + k, 4)
-        to_y.append(copies.send(w_out.at[other], w_all.at[:, y, x, core], y_peer[k]))
-    for h in range(2):
-        w_all[h, y, x, core] = w_out[y, h]
-    for copy in to_y:
-        copy.wait_recv()
-    mine = w_all.at[:, :, x, core]
-    to_x = [(k, copies.send(mine, mine, x_peer[k])) for k in (2, 1, 3)]
-    to_core = [copies.send(mine, mine, sibling)]
-    for k, copy in (to_x[1], to_x[2], to_x[0]):
-        copy.wait_recv()
-        theirs = w_all.at[:, :, lax.rem(x + 4 - k, 4), core]
-        to_core.append(copies.send(theirs, theirs, sibling))
-    for copy in to_core:
-        copy.wait_recv()
-
-    for h in range(2):
+    to_y, to_group, to_z = {}, {}, []
+
+    def head_columns(h):
+        to_y[h] = [
+            copies.send(
+                w_out.at[h, lax.rem(y + k, 4)], w_all.at[h, y, x, core], y_peer[k]
+            )
+            for k in (2, 1, 3)
+        ]
+        w_all[h, y, x, core] = w_out[h, y]
+
+    def share_weights(h):
+        for copy in to_y[h]:
+            copy.wait_recv()
+        mine = w_all.at[h, :, x, core]
+        to_group[h] = [copies.send(mine, mine, device) for device in group[1:] + group[:1]]
+
+    def send_keys(h):
+        for copy in to_group[h]:
+            copy.wait_recv()
         key_part[h] = jnp.dot(
             normed[...], w_all[h].reshape(512, 128), preferred_element_type=F32
         ).reshape(8, 16, 128)
-    to_z = []
-    for k in (8, 7, 9, 6, 10, 5, 11, 4, 12, 3, 13, 2, 14, 1, 15):
-        other = z_of(k)
-        to_z.append(
+        away = zh if h == 0 else 1 - zh
+        if h == 1:
             copies.send(
-                key_part.at[lax.div(other, 8), lax.rem(other, 8)], key_in.at[z], z_peer(k)
+                key_part.at[1 - zh, zl, pl.ds(0, 12)],
+                key_in.at[z, pl.ds(0, 12)],
+                at(zh_=1 - zh),
+                key_sems.at[14],
             )
+        for k in (4, 3, 5, 2, 6, 1, 7):
+            other = lax.rem(zl + k, 8)
+            copies.send(
+                key_part.at[h, other, pl.ds(0, 12)],
+                key_in.at[z, pl.ds(0, 12)],
+                at(zl_=other, zh_=h),
+                key_sems.at[away * 7 + k - 1],
+            )
+
+    def finish():
+        key_in[z] = key_part[zh, zl]
+        for number in range(15):
+            pltpu.make_async_remote_copy(
+                src_ref=key_part.at[0, 0, pl.ds(0, 12)],
+                dst_ref=key_in.at[0, pl.ds(0, 12)],
+                send_sem=send_sems.at[0],
+                recv_sem=key_sems.at[number],
+                device_id=sibling,
+                device_id_type=MESH,
+            ).wait_recv()
+        total = key_in[0, 0:12]
+        for k in range(1, 16):
+            total = total + key_in[k, 0:12]
+        keys_out[...] = jnp.zeros_like(keys_out)
+        keys_out[0:12, :] = total
+        keys = keys_out[...].astype(BF16)
+
+        new = (
+            lax.dot_general(
+                q32[...].astype(BF16), keys, (((1,), (1,)), ((), ())), preferred_element_type=F32
+            )
+            * scale
         )
-    key_in[z] = key_part[zh, zl]
-    for copy in to_z:
-        copy.wait_recv()
-    keys = key_in[0]
-    for k in range(1, 16):
-        keys = keys + key_in[k]
-    keys = keys.astype(BF16)
-    keys_out[...] = keys.astype(F32)
-
-    new = (
-        lax.dot_general(
-            q32[...].astype(BF16), keys, (((1,), (1,)), ((), ())), preferred_element_type=F32
-        )
-        * scale
+        row = lax.broadcasted_iota(jnp.int32, (128, 16), 0)
+        column = lax.broadcasted_iota(jnp.int32, (128, 16), 1)
+        same_row = (row // 32) == (column % 4)
+        earlier = (column // 4) <= ((row % 32) // 8)
+        new = jnp.where(same_row & earlier & (column < 12), new, -jnp.inf)
+        top = jnp.maximum(old_top[...], jnp.max(new, axis=1, keepdims=True))
+        fade = jnp.exp(old_top[...] - top)
+        new = jnp.exp(new - top)
+        total = old_sum[...] * fade + jnp.sum(new, axis=1, keepdims=True)
+        new_probs = (new / total).astype(BF16)
+        share = fade / total
+        attended = jnp.dot(new_probs, sv32[...].astype(BF16), preferred_element_type=F32)
+        for r in range(4):
+            rows = slice(32 * r, 32 * r + 32)
+            probs = (old_exp[rows, :] * share[rows]).astype(BF16)
+            att = attended[rows] + jnp.dot(probs, cv_v[r, 0], preferred_element_type=F32)
+            for s in range(3):
+                att_out[s, r] = att[8 * s : 8 * s + 8]
+
+    def adam_loads():
+        for number in range(7, 11):
+            loads[number].wait()
+
+    schedule = (
+        (ring_first, 0),
+        (hop, 5),
+        (ring_first, 1),
+        (ring_second, 0),
+        (hop, 6),
+        (line_pair, 0),
+        (ring_first, 2),
+        (hop, 7),
+        (send_rows,),
+        (ring_second, 1),
+        (line_quad, 0),
+        (line_pair, 1),
+        (ring_first, 3),
+        (ring_second, 2),
+        (line_quad, 1),
+        (line_pair, 2),
+        (ring_second, 3),
+        (adam_loads,),
+        (update, 0),
+        (line_quad, 2),
+        (line_pair, 3),
+        (update, 1),
+        (head_columns, 0),
+        (line_quad, 3),
+        (share_weights, 0),
+        (make_normed,),
+        (update, 2),
+        (send_keys, 0),
+        (update, 3),
+        (head_columns, 1),
+        (old_scores,),
+        (share_weights, 1),
+        (send_keys, 1),
+        (finish,),
     )
-    row = lax.broadcasted_iota(jnp.int32, (128, 16), 0)
-    column = lax.broadcasted_iota(jnp.int32, (128, 16), 1)
-    same_row = (row // 32) == (column % 4)
-    earlier = (column // 4) <= ((row % 32) // 8)
-    new = jnp.where(same_row & earlier & (column < 12), new, -jnp.inf)
-    top = jnp.maximum(old_top[...], jnp.max(new, axis=1, keepdims=True))
-    fade = jnp.exp(old_top[...] - top)
-    new = jnp.exp(new - top)
-    total = old_sum[...] * fade + jnp.sum(new, axis=1, keepdims=True)
-    new_probs = (new / total).astype(BF16)
-    share = fade / total
-    attended = jnp.dot(new_probs, sv32[...].astype(BF16), preferred_element_type=F32)
-    for r in range(4):
-        rows = slice(32 * r, 32 * r + 32)
-        probs = (old_exp[rows, :] * share[rows]).astype(BF16)
-        att = attended[rows] + jnp.dot(probs, cv_v[r, 0], preferred_element_type=F32)
-        for s in range(3):
-            att_out[s, r] = att[8 * s : 8 * s + 8]
+    for do, *chunk in schedule:
+        do(*chunk)
 
     for copy in copies.made:
         copy.wait_send()
     assert len(copies.made) == N_COPIES, len(copies.made)
+
+
+def store(
+    master_v, one_v, two_v, keys_v, att_v, step_v, master, one, two, keys, decoded, keys_b, dec_b, sems
+):
+    copies = []
+
+    def start(src, dst):
+        copies.append(pltpu.make_async_copy(src, dst, sems.at[len(copies)]))
+        copies[-1].start()
+
+    start(master_v, master)
+    start(one_v, one)
+    start(two_v, two)
+    for s in range(3):
+        keys_b[s] = keys_v[4 * s : 4 * s + 4, :].astype(BF16)
+    start(keys_b, keys)
+    for s in range(3):
+        for g in range(8):
+            columns = slice(128 * g, 128 * g + 128)
+            dec_b[s, :, columns] = (
+                step_v[s, :, columns].astype(F32) + att_v[s, :, g, :]
+            ).astype(BF16)
+    start(dec_b, decoded)
+    for copy in copies:
+        copy.wait()
 
 
 def body(
@@ -424,19 +498,20 @@
     cache_lengths,
     norm_gain,
 ):
-    anywhere = pl.BlockSpec(memory_space=pl.ANY)
+    hbm = pl.BlockSpec(memory_space=pltpu.HBM)
     vmem = pl.BlockSpec(memory_space=pltpu.VMEM)
     owned = jax.ShapeDtypeStruct(master.shape, F32)
-    new_master, new_one, new_two, keys, attended = pl.pallas_call(
+    owned_v = pltpu.VMEM(master.shape, F32)
+    results = pl.pallas_call(
         kernel,
         out_shape=(
-            owned,
-            owned,
-            owned,
-            jax.ShapeDtypeStruct((16, 128), F32),
-            jax.ShapeDtypeStruct((3, 4, 8, 128), F32),
+            owned_v,
+            owned_v,
+            owned_v,
+            pltpu.VMEM((16, 128), F32),
+            pltpu.VMEM((3, 4, 8, 128), F32),
         ),
-        in_specs=[anywhere] * 10 + [pl.BlockSpec(memory_space=pltpu.SMEM), anywhere],
+        in_specs=[hbm] * 10 + [pl.BlockSpec(memory_space=pltpu.SMEM), hbm],
         out_specs=(vmem,) * 5,
         scratch_shapes=[
             pltpu.VMEM((1024, 1024), BF16),
@@ -444,7 +519,7 @@
             pltpu.VMEM((3, 1, 16, 1024), F32),
             pltpu.VMEM((3, 4, 1024), BF16),
             pltpu.VMEM((3, 4, 8, 128), BF16),
-            pltpu.VMEM((3, 4, 1, 128), BF16),
+            pltpu.VMEM((3, 4, 128), BF16),
             pltpu.VMEM((4, 1, 512, 128), BF16),
             pltpu.VMEM((4, 1, 512, 128), BF16),
             pltpu.VMEM((64, 128), F32),
@@ -463,7 +538,7 @@
             pltpu.VMEM((8, 4, 16, 128), BF16),
             pltpu.VMEM((16, 1, 128), F32),
             pltpu.VMEM((128, 512), BF16),
-            pltpu.VMEM((4, 2, 16, 128), BF16),
+            pltpu.VMEM((2, 4, 16, 128), BF16),
             pltpu.VMEM((2, 4, 4, 2, 16, 128), BF16),
             pltpu.VMEM((2, 8, 16, 128), F32),
             pltpu.VMEM((16, 16, 128), F32),
@@ -475,28 +550,52 @@
             pltpu.SemaphoreType.DMA((11,)),
             pltpu.SemaphoreType.DMA((N_COPIES,)),
             pltpu.SemaphoreType.DMA((N_COPIES,)),
+            pltpu.SemaphoreType.DMA((15,)),
+            pltpu.SemaphoreType.REGULAR((7, 2)),
         ],
         compiler_params=pltpu.CompilerParams(
-            collective_id=0, has_side_effects=True, vmem_limit_bytes=48 << 20
+            collective_id=0, has_side_effects=True, vmem_limit_bytes=40 << 20
         ),
         name="adam_decode",
     )(
-        train_inputs,
-        key_cotangent,
-        master,
-        moment_one,
-        moment_two,
-        step_inputs,
-        decode_queries,
-        step_values,
-        cache_keys,
-        cache_values,
+        *(
+            pltpu.with_memory_space_constraint(array, pltpu.HBM)
+            for array in (
+                train_inputs,
+                key_cotangent,
+                master,
+                moment_one,
+                moment_two,
+                step_inputs,
+                decode_queries,
+                step_values.reshape(3, 4, 128),
+                cache_keys,
+                cache_values,
+            )
+        ),
         cache_lengths,
-        norm_gain.reshape(64, 128),
+        pltpu.with_memory_space_constraint(norm_gain.reshape(64, 128), pltpu.HBM),
     )
-    new_keys = keys[:12].reshape(step_values.shape).astype(BF16)
-    decoded = (step_inputs.astype(F32) + attended.reshape(step_inputs.shape)).astype(BF16)
-    return new_master, new_one, new_two, new_keys, decoded
+    new_master, new_one, new_two, new_keys, decoded = pl.pallas_call(
+        store,
+        out_shape=(
+            owned,
+            owned,
+            owned,
+            jax.ShapeDtypeStruct((3, 4, 128), BF16),
+            jax.ShapeDtypeStruct(step_inputs.shape, BF16),
+        ),
+        in_specs=[vmem] * 6,
+        out_specs=(hbm,) * 5,
+        scratch_shapes=[
+            pltpu.VMEM((3, 4, 128), BF16),
+            pltpu.VMEM((3, 4, 1024), BF16),
+            pltpu.SemaphoreType.DMA((5,)),
+        ],
+        compiler_params=pltpu.CompilerParams(vmem_limit_bytes=40 << 20),
+        name="store_results",
+    )(*results, step_inputs)
+    return new_master, new_one, new_two, new_keys.reshape(step_values.shape), decoded
 
 
 def solution(mesh):

time: 87.9 us -> 69 us (0.78)
  local copies, waits for them, and re-layouts: 13.9 us -> 0.65 us
  Pallas kernels: 72 us -> 67.5 us
    unnamed x28 -> x4, local copies, waits for them, and re-layouts: 13.2 us -> 0.65 us
    pallas_call x1 -> x2, Pallas kernels: 72 us -> 67.5 us  [the longest x1 66.8 us: body(): pl.pallas_call(kernel, out_shape=(owned_v, owned_v, owned_v, pltpu.VMEM((...]
where the time goes in v2:
time: 69 us; the launch traced here: 68.8 us
  Pallas kernels  67.5 us (98%)
    pallas_call x1, Pallas kernels, body(): pl.pallas_call(kernel, out_shape=(owned_v, owned_v, owned_v, pltpu.VMEM((...  66.8 us

profile of v2, /device:TPU:1, one launch (start us, length us, event | category | flops | bytes accessed | tf_op | source)
XLA Modules:
  0.0 68.8 jit_solution(15334052896400179076)
XLA Ops:
  0.6 0.0 copy-start.1
  0.6 0.6 copy-done.1
  1.3 0.0 copy-start
  1.3 66.8 %adam_decode.1 = (f32[1,16,1024]{2,1,0:T(8,128)S(1)}, f32[1,16,1024]{2,1,0:T(8,128)S(1)}, f32[1,16,1024]{2,1,0:T(8,128)S(1)}, f32[16,128]{1,0:T(8,128)S(1)}, f32[3,4,8,128]{3,2,1,0:T(8,128)S(1)}) custom-call(bf16[1024,1024]{1,0:T(8,128)(2,1)} %x_hbm.1, bf16[1024,1024]{1,0:T(8,128)(2,1)} %c_hbm.1, f32[1,16,1024]{2,1,0:T(8,128)} %master_hbm.1, ...), custom_call_target="tpu_custom_call" | custom-call | tf_op jit(solution)/shard_map/adam_decode/pallas_call | solution.py:505
  68.1 0.0 copy-done
  68.1 0.7 %store_results.1 = (f32[1,16,1024]{2,1,0:T(8,128)}, f32[1,16,1024]{2,1,0:T(8,128)}, f32[1,16,1024]{2,1,0:T(8,128)}, bf16[3,4,128]{2,1,0:T(4,128)(2,1)}, bf16[3,4,1024]{2,1,0:T(4,128)(2,1)}) custom-call(f32[1,16,1024]{2,1,0:T(8,128)S(1)} %get-tuple-element.15.master_v, f32[1,16,1024]{2,1,0:T(8,128)S(1)} %get-tuple-element.16.one_v, ...), custom_call_target="tpu_custom_call" | custom-call | tf_op jit(solution)/shard_map/store_results/pallas_call | solution.py:579
Async XLA Ops:
  0.6 0.7 copy-start.1
  1.3 66.8 %copy-start = (bf16[3,4,1024]{2,1,0:T(4,128)(2,1)S(1)}, bf16[3,4,1024]{2,1,0:T(4,128)(2,1)}, u32[]{:S(2)}) copy-start(bf16[3,4,1024]{2,1,0:T(4,128)(2,1)} %step_v.1) | copy-start | bytes 73732

commit v3 on v2

--- a/solution.py
+++ b/solution.py
@@ -17,27 +17,27 @@
 BF16 = jnp.bfloat16
 
 
-class Copies:
-    def __init__(self, send_sems, recv_sems):
-        self.send_sems, self.recv_sems = send_sems, recv_sems
-        self.made = []
-
-    def send(self, src, dst, device, recv_sem=None):
-        number = len(self.made)
-        copy = pltpu.make_async_remote_copy(
-            src_ref=src,
-            dst_ref=dst,
-            send_sem=self.send_sems.at[number],
-            recv_sem=self.recv_sems.at[number] if recv_sem is None else recv_sem,
-            device_id=device,
-            device_id_type=MESH,
-        )
-        copy.start()
-        self.made.append(copy)
-        return copy
-
-
-N_COPIES = 25 + 11 * CHUNKS + 35
+class Sems:
+    def __init__(self, sems):
+        self.sems, self.used = sems, 0
+
+    def new(self):
+        self.used += 1
+        return self.sems.at[self.used - 1]
+
+
+def remote(src, dst, send_sem, recv_sem, device):
+    return pltpu.make_async_remote_copy(
+        src_ref=src,
+        dst_ref=dst,
+        send_sem=send_sem,
+        recv_sem=recv_sem,
+        device_id=device,
+        device_id_type=MESH,
+    )
+
+
+N_SEMS = 27 + 7 * CHUNKS
 
 
 def kernel(
@@ -91,10 +91,7 @@
     old_top,
     old_sum,
     sv32,
-    local_sems,
-    send_sems,
-    recv_sems,
-    key_sems,
+    copy_sems,
     far_sems,
 ):
     f, t = lax.axis_index("fsdp"), lax.axis_index("tp")
@@ -122,6 +119,8 @@
         other = z_of(k)
         return at(zl_=lax.rem(other, 8), zh_=lax.div(other, 8))
 
+    sems = Sems(copy_sems)
+
     barrier = pltpu.get_barrier_semaphore()
     group = [sibling] + [
         at(x_=lax.rem(x + k, 4), core_=c_) for k in (2, 1, 3) for c_ in (core, 1 - core)
@@ -130,27 +129,29 @@
     for partner in partners:
         pl.semaphore_signal(barrier, inc=1, device_id=partner, device_id_type=MESH)
 
-    loads = []
-    for number, (src, dst) in enumerate(
-        (
-            (x_hbm, x_v),
-            (c_hbm, c_v),
-            (step_hbm, step_v),
-            (query_hbm, query_v),
-            (ck_hbm, ck_v),
-            (cv_hbm, cv_v),
-            (value_hbm, value_v),
-            (gain_hbm, gain_v),
-            (master_hbm, adam_v.at[0]),
-            (one_hbm, adam_v.at[1]),
-            (two_hbm, adam_v.at[2]),
-        )
-    ):
-        load = pltpu.make_async_copy(src, dst, local_sems.at[number])
-        load.start()
-        loads.append(load)
-
-    loads[2].wait()
+    def load(pairs, whole=None):
+        sem = sems.new()
+        for src, dst in pairs:
+            pltpu.make_async_copy(src, dst, sem).start()
+        return pltpu.make_async_copy(*(whole or pairs[0]), sem)
+
+    step_load = load([(step_hbm, step_v)])
+    x_load = load([(x_hbm, x_v)])
+    c_loads = []
+    for j in range(CHUNKS):
+        columns = slice(j * CW, (j + 1) * CW)
+        c_loads.append(load([(c_hbm.at[:, columns], c_v.at[:, columns])]))
+    score_loads = [
+        load([pair])
+        for pair in ((query_hbm, query_v), (ck_hbm, ck_v), (cv_hbm, cv_v), (value_hbm, value_v))
+    ]
+    gain_load = load([(gain_hbm, gain_v)])
+    adam_load = load(
+        [(ref, adam_v.at[k]) for k, ref in enumerate((master_hbm, one_hbm, two_hbm))],
+        (adam_v, adam_v),
+    )
+
+    step_load.wait()
     rows32[...] = jnp.zeros_like(rows32)
     for s in range(3):
         rows32[4 * s : 4 * s + 4, :] = step_v[s].astype(F32)
@@ -158,25 +159,38 @@
         rows_y[y, k] = rows32[:, 128 * k : 128 * k + 128].astype(BF16)
 
     pl.semaphore_wait(barrier, len(partners))
-    copies = Copies(send_sems, recv_sems)
+    sent = []
+
+    def sender(whole):
+        sem = sems.new()
+        sent.append(remote(whole, whole, sem, sem, sibling))
+        return sem
+
+    def arrival(whole):
+        sem = sems.new()
+        return sem, remote(whole, whole, sem, sem, sibling)
 
     def hop(d):
         if d > 0:
-            pl.semaphore_wait(far_sems.at[d - 1, 0], 1)
-            pl.semaphore_wait(far_sems.at[d - 1, 1], 1)
+            pl.semaphore_wait(far_sems.at[d - 1], 2)
         if d < 7:
-            for side, partner in enumerate((z_peer(1), z_peer(15))):
+            for partner in (z_peer(1), z_peer(15)):
                 pl.semaphore_signal(
-                    far_sems.at[d, side], inc=1, device_id=partner, device_id_type=MESH
+                    far_sems.at[d], inc=1, device_id=partner, device_id_type=MESH
                 )
 
     hop(0)
-    own_rows = [copies.send(rows_y.at[y], rows_y.at[y], y_peer[k]) for k in (2, 1, 3)]
-
-    loads[0].wait()
-    loads[1].wait()
-    swaps = []
-    for j in range(CHUNKS):
+    own_sent, (own_sem, own_rows) = sender(rows_y.at[0:3]), arrival(rows_y.at[0:3])
+    for k in (2, 1, 3):
+        remote(rows_y.at[y], rows_y.at[y], own_sent, own_sem, y_peer[k]).start()
+
+    swap_sent = sender(part.at[:, 1 - core])
+    swaps = [arrival(part_in.at[j]) for j in range(CHUNKS)]
+
+    def local_term(j):
+        if j == 0:
+            x_load.wait()
+        c_loads[j].wait()
         term = lax.dot_general(
             x_v[...],
             c_v[:, j * CW : (j + 1) * CW],
@@ -185,12 +199,20 @@
         ).reshape(8, 4, 2, 16, CW)
         part[j, 0] = term[:, :, 0]
         part[j, 1] = term[:, :, 1]
-        swaps.append(copies.send(part.at[j, 1 - core], part_in.at[j], sibling))
-        hop(j + 1)
+        remote(part.at[j, 1 - core], part_in.at[j], swap_sent, swaps[j][0], sibling).start()
 
     xp, xo, xm = (lax.rem(x + k, 4) for k in (1, 2, 3))
     low, high = slice(0, 4), slice(4, 8)
-    ring, pairs, quads = {}, {}, {}
+    ring_sent = sender(ring_out)
+    ring = [
+        [arrival(ring_in.at[j, 0]), arrival(ring_in.at[j, 1])]
+        + [arrival(ring_in.at[j, 2:6])] * 4
+        for j in range(CHUNKS)
+    ]
+    pair_sent = sender(pair_out)
+    pairs = [arrival(pair_in.at[j]) for j in range(CHUNKS)]
+    quad_sent = sender(quad_out.at[:, 0:3])
+    quads = [arrival(quad_in.at[j]) for j in range(CHUNKS)]
     parity, quad = lax.rem(zl, 2), lax.div(zl, 2)
 
     def chip_sum(j, half, target):
@@ -198,24 +220,25 @@
 
     def ring_send(j, number, value, device):
         ring_out[j, number] = value.astype(BF16)
-        ring[j, number] = copies.send(ring_out.at[j, number], ring_in.at[j, number], device)
+        remote(
+            ring_out.at[j, number], ring_in.at[j, number], ring_sent, ring[j][number][0], device
+        ).start()
 
     def ring_first(j):
-        swaps[j].wait_recv()
+        swaps[j][1].wait_recv()
         ring_send(j, 0, chip_sum(j, low, xo), x_peer[1])
         ring_send(j, 1, chip_sum(j, high, xo), x_peer[3])
         ring_send(j, 2, chip_sum(j, high, xp), x_peer[1])
         ring_send(j, 3, chip_sum(j, low, xm), x_peer[3])
 
     def ring_second(j):
-        ring[j, 0].wait_recv()
+        ring[j][0][1].wait_recv()
         ring_send(j, 4, chip_sum(j, low, xp) + ring_in[j, 0].astype(F32), x_peer[1])
-        ring[j, 1].wait_recv()
+        ring[j][1][1].wait_recv()
         ring_send(j, 5, chip_sum(j, high, xm) + ring_in[j, 1].astype(F32), x_peer[3])
 
     def line_pair(j):
-        for number in (2, 3, 4, 5):
-            ring[j, number].wait_recv()
+        ring[j][2][1].wait_recv()
         line_sum[j, low] = (
             chip_sum(j, low, x) + ring_in[j, 3].astype(F32) + ring_in[j, 4].astype(F32)
         )
@@ -224,25 +247,28 @@
         )
         for q in range(4):
             pair_out[j, q] = line_sum[j, 2 * q + 1 - parity].astype(BF16)
-        pairs[j] = copies.send(
-            pair_out.at[j], pair_in.at[j], at(zl_=zl + 1 - 2 * parity)
-        )
+        remote(
+            pair_out.at[j], pair_in.at[j], pair_sent, pairs[j][0], at(zl_=zl + 1 - 2 * parity)
+        ).start()
 
     def line_quad(j):
-        pairs[j].wait_recv()
+        pairs[j][1].wait_recv()
         for q in range(4):
             total = line_sum[j, 2 * q + parity] + pair_in[j, q].astype(F32)
             quad_sum[j, q] = total
             quad_out[j, q] = total.astype(BF16)
         for k in (2, 3, 1):
             other = lax.rem(quad + k, 4)
-            quads[j, k] = copies.send(
-                quad_out.at[j, other], quad_in.at[j, k - 1], at(zl_=2 * other + parity)
-            )
+            remote(
+                quad_out.at[j, other],
+                quad_in.at[j, k - 1],
+                quad_sent,
+                quads[j][0],
+                at(zl_=2 * other + parity),
+            ).start()
 
     def update(j):
-        for k in (1, 2, 3):
-            quads[j, k].wait_recv()
+        quads[j][1].wait_recv()
         gradient = quad_sum[j, quad]
         for k in (1, 2, 3):
             gradient = gradient + quad_in[j, k - 1].astype(F32)
@@ -262,14 +288,19 @@
 
     lane = lax.broadcasted_iota(jnp.int32, (16, 128), 1)
     diagonal = lane == lax.broadcasted_iota(jnp.int32, (16, 128), 0)
-    spread, rows_sent = {}, {}
+    rows_sent, (rows_sem, rows_here) = sender(rows_z.at[0:7]), arrival(rows_z.at[0:7])
+    squares_sent, (squares_sem, squares_here) = (
+        sender(squares.at[0:15]),
+        arrival(squares.at[0:15]),
+    )
 
     def send_rows():
-        for copy in own_rows:
-            copy.wait_recv()
+        own_rows.wait_recv()
         for k in (4, 3, 5, 2, 6, 1, 7):
             other = lax.rem(zl + k, 8)
-            rows_sent[k] = copies.send(rows_y.at[:, other], rows_z.at[zl], at(zl_=other))
+            remote(
+                rows_y.at[:, other], rows_z.at[zl], rows_sent, rows_sem, at(zl_=other)
+            ).start()
         total = jnp.zeros((16, 128), F32)
         for q in range(4):
             for k in range(8):
@@ -278,15 +309,14 @@
         column = jnp.sum(total, axis=1, keepdims=True)
         squares[z] = jnp.sum(jnp.where(diagonal, column, 0.0), axis=0, keepdims=True)
         for k in (8, 7, 9, 6, 10, 5, 11, 4, 12, 3, 13, 2, 14, 1, 15):
-            spread[k] = copies.send(squares.at[z], squares.at[z], z_peer(k))
+            remote(squares.at[z], squares.at[z], squares_sent, squares_sem, z_peer(k)).start()
         for q in range(4):
             rows_z[zl, q] = rows_y[q, zl]
 
     def make_normed():
-        for k in range(1, 16):
-            spread[k].wait_recv()
-        for k in range(1, 8):
-            rows_sent[k].wait_recv()
+        gain_load.wait()
+        squares_here.wait_recv()
+        rows_here.wait_recv()
         for s in range(8):
             both = squares[s] + squares[s + 8]
             column = jnp.sum(jnp.where(diagonal, both, 0.0), axis=1, keepdims=True)
@@ -299,8 +329,8 @@
     scale = 1.0 / 128.0**0.5
 
     def old_scores():
-        for number in (3, 4, 5, 6):
-            loads[number].wait()
+        for copy in score_loads:
+            copy.wait()
         q32[...] = jnp.zeros_like(q32)
         for s in range(3):
             for r in range(4):
@@ -327,57 +357,53 @@
             old_top[rows, :] = top
             old_sum[rows, :] = jnp.sum(weight, axis=1, keepdims=True)
 
-    to_y, to_group, to_z = {}, {}, []
+    to_y_sent = sender(w_out.at[:, 0:3])
+    to_y = [arrival(w_out.at[h, 0:3]) for h in range(2)]
+    shared_sent = [sender(rows_z.at[0:7]) for h in range(2)]
+    shared = [arrival(rows_z.at[0:7]) for h in range(2)]
+    keys_sent = sender(key_in.at[0:15, pl.ds(0, 12)])
+    keys_sem, keys_here = arrival(key_in.at[0:15, pl.ds(0, 12)])
 
     def head_columns(h):
-        to_y[h] = [
-            copies.send(
-                w_out.at[h, lax.rem(y + k, 4)], w_all.at[h, y, x, core], y_peer[k]
-            )
-            for k in (2, 1, 3)
-        ]
+        for k in (2, 1, 3):
+            remote(
+                w_out.at[h, lax.rem(y + k, 4)],
+                w_all.at[h, y, x, core],
+                to_y_sent,
+                to_y[h][0],
+                y_peer[k],
+            ).start()
         w_all[h, y, x, core] = w_out[h, y]
 
     def share_weights(h):
-        for copy in to_y[h]:
-            copy.wait_recv()
+        to_y[h][1].wait_recv()
         mine = w_all.at[h, :, x, core]
-        to_group[h] = [copies.send(mine, mine, device) for device in group[1:] + group[:1]]
+        for device in group[1:] + group[:1]:
+            remote(mine, mine, shared_sent[h], shared[h][0], device).start()
 
     def send_keys(h):
-        for copy in to_group[h]:
-            copy.wait_recv()
+        shared[h][1].wait_recv()
         key_part[h] = jnp.dot(
             normed[...], w_all[h].reshape(512, 128), preferred_element_type=F32
         ).reshape(8, 16, 128)
-        away = zh if h == 0 else 1 - zh
+
+        def send(half, line):
+            remote(
+                key_part.at[half, line, pl.ds(0, 12)],
+                key_in.at[z, pl.ds(0, 12)],
+                keys_sent,
+                keys_sem,
+                at(zl_=line, zh_=half),
+            ).start()
+
         if h == 1:
-            copies.send(
-                key_part.at[1 - zh, zl, pl.ds(0, 12)],
-                key_in.at[z, pl.ds(0, 12)],
-                at(zh_=1 - zh),
-                key_sems.at[14],
-            )
+            send(1 - zh, zl)
         for k in (4, 3, 5, 2, 6, 1, 7):
-            other = lax.rem(zl + k, 8)
-            copies.send(
-                key_part.at[h, other, pl.ds(0, 12)],
-                key_in.at[z, pl.ds(0, 12)],
-                at(zl_=other, zh_=h),
-                key_sems.at[away * 7 + k - 1],
-            )
+            send(h, lax.rem(zl + k, 8))
 
     def finish():
         key_in[z] = key_part[zh, zl]
-        for number in range(15):
-            pltpu.make_async_remote_copy(
-                src_ref=key_part.at[0, 0, pl.ds(0, 12)],
-                dst_ref=key_in.at[0, pl.ds(0, 12)],
-                send_sem=send_sems.at[0],
-                recv_sem=key_sems.at[number],
-                device_id=sibling,
-                device_id_type=MESH,
-            ).wait_recv()
+        keys_here.wait_recv()
         total = key_in[0, 0:12]
         for k in range(1, 16):
             total = total + key_in[k, 0:12]
@@ -411,40 +437,47 @@
                 att_out[s, r] = att[8 * s : 8 * s + 8]
 
     def adam_loads():
-        for number in range(7, 11):
-            loads[number].wait()
+        adam_load.wait()
 
     schedule = (
+        (local_term, 0),
+        (hop, 1),
+        (local_term, 1),
+        (hop, 2),
         (ring_first, 0),
+        (local_term, 2),
+        (hop, 3),
+        (ring_first, 1),
+        (local_term, 3),
+        (hop, 4),
+        (ring_second, 0),
+        (ring_first, 2),
         (hop, 5),
-        (ring_first, 1),
-        (ring_second, 0),
+        (ring_second, 1),
+        (line_pair, 0),
+        (ring_first, 3),
         (hop, 6),
-        (line_pair, 0),
-        (ring_first, 2),
+        (ring_second, 2),
+        (line_pair, 1),
         (hop, 7),
+        (line_quad, 0),
+        (ring_second, 3),
+        (line_pair, 2),
+        (line_quad, 1),
+        (line_pair, 3),
+        (line_quad, 2),
+        (line_quad, 3),
         (send_rows,),
-        (ring_second, 1),
-        (line_quad, 0),
-        (line_pair, 1),
-        (ring_first, 3),
-        (ring_second, 2),
-        (line_quad, 1),
-        (line_pair, 2),
-        (ring_second, 3),
         (adam_loads,),
         (update, 0),
-        (line_quad, 2),
-        (line_pair, 3),
         (update, 1),
         (head_columns, 0),
-        (line_quad, 3),
+        (update, 2),
         (share_weights, 0),
-        (make_normed,),
-        (update, 2),
-        (send_keys, 0),
         (update, 3),
         (head_columns, 1),
+        (make_normed,),
+        (send_keys, 0),
         (old_scores,),
         (share_weights, 1),
         (send_keys, 1),
@@ -453,9 +486,9 @@
     for do, *chunk in schedule:
         do(*chunk)
 
-    for copy in copies.made:
+    for copy in sent:
         copy.wait_send()
-    assert len(copies.made) == N_COPIES, len(copies.made)
+    assert sems.used == N_SEMS, sems.used
 
 
 def store(
@@ -547,11 +580,8 @@
             pltpu.VMEM((128, 1), F32),
             pltpu.VMEM((128, 1), F32),
             pltpu.VMEM((16, 128), F32),
-            pltpu.SemaphoreType.DMA((11,)),
-            pltpu.SemaphoreType.DMA((N_COPIES,)),
-            pltpu.SemaphoreType.DMA((N_COPIES,)),
-            pltpu.SemaphoreType.DMA((15,)),
-            pltpu.SemaphoreType.REGULAR((7, 2)),
+            pltpu.SemaphoreType.DMA((N_SEMS,)),
+            pltpu.SemaphoreType.REGULAR((7,)),
         ],
         compiler_params=pltpu.CompilerParams(
             collective_id=0, has_side_effects=True, vmem_limit_bytes=40 << 20

time: 69 us -> 61 us (0.88)
  Pallas kernels: 67.5 us -> 59.5 us
    pallas_call x1, Pallas kernels: 66.8 us -> 58.8 us  [body(): pl.pallas_call(kernel, out_shape=(owned_v, owned_v, owned_v, pltpu.VMEM((...]
where the time goes in v3:
time: 61 us; the launch traced here: 60.8 us
  Pallas kernels  59.5 us (98%)
  between operations  0.66 us (1%)
  local copies, waits for them, and re-layouts  0.65 us (1%)
    pallas_call x1, Pallas kernels, body(): pl.pallas_call(kernel, out_shape=(owned_v, owned_v, owned_v, pltpu.VMEM((...  58.8 us

profile of v3, /device:TPU:1, one launch (start us, length us, event | category | flops | bytes accessed | tf_op | source)
XLA Modules:
  0.0 60.8 jit_solution(250581432570896324)
XLA Ops:
  0.6 0.0 copy-start.1
  0.6 0.6 %copy-done.1 = s32[4]{0:T(128)S(1)} copy-done((s32[4]{0:T(128)S(1)}, s32[4]{0:T(128)}, u32[]{:S(2)}) %copy-start.1) | copy-done | bytes 40
  1.3 0.0 copy-start
  1.3 58.8 %adam_decode.1 = (f32[1,16,1024]{2,1,0:T(8,128)S(1)}, f32[1,16,1024]{2,1,0:T(8,128)S(1)}, f32[1,16,1024]{2,1,0:T(8,128)S(1)}, f32[16,128]{1,0:T(8,128)S(1)}, f32[3,4,8,128]{3,2,1,0:T(8,128)S(1)}) custom-call(bf16[1024,1024]{1,0:T(8,128)(2,1)} %x_hbm.1, bf16[1024,1024]{1,0:T(8,128)(2,1)} %c_hbm.1, f32[1,16,1024]{2,1,0:T(8,128)} %master_hbm.1, ...), custom_call_target="tpu_custom_call" | custom-call | tf_op jit(solution)/shard_map/adam_decode/pallas_call | solution.py:538
  60.1 0.0 copy-done
  60.1 0.7 %store_results.1 = (f32[1,16,1024]{2,1,0:T(8,128)}, f32[1,16,1024]{2,1,0:T(8,128)}, f32[1,16,1024]{2,1,0:T(8,128)}, bf16[3,4,128]{2,1,0:T(4,128)(2,1)}, bf16[3,4,1024]{2,1,0:T(4,128)(2,1)}) custom-call(f32[1,16,1024]{2,1,0:T(8,128)S(1)} %get-tuple-element.15.master_v, f32[1,16,1024]{2,1,0:T(8,128)S(1)} %get-tuple-element.16.one_v, ...), custom_call_target="tpu_custom_call" | custom-call | tf_op jit(solution)/shard_map/store_results/pallas_call | solution.py:609
Async XLA Ops:
  0.6 0.7 %copy-start.1 = (s32[4]{0:T(128)S(1)}, s32[4]{0:T(128)}, u32[]{:S(2)}) copy-start(s32[4]{0:T(128)} %lengths.1) | copy-start | bytes 52
  1.3 58.8 %copy-start = (bf16[3,4,1024]{2,1,0:T(4,128)(2,1)S(1)}, bf16[3,4,1024]{2,1,0:T(4,128)(2,1)}, u32[]{:S(2)}) copy-start(bf16[3,4,1024]{2,1,0:T(4,128)(2,1)} %step_v.1) | copy-start | bytes 73732

commit v4 on v3

--- a/solution.py
+++ b/solution.py
@@ -37,7 +37,7 @@
     )
 
 
-N_SEMS = 27 + 7 * CHUNKS
+N_SEMS = 25 + 7 * CHUNKS
 
 
 def kernel(
@@ -51,7 +51,7 @@
     value_hbm,
     ck_hbm,
     cv_hbm,
-    lengths,
+    lengths_hbm,
     gain_hbm,
     new_master,
     new_one,
@@ -67,7 +67,9 @@
     ck_v,
     cv_v,
     gain_v,
+    lengths,
     part,
+    part_out,
     part_in,
     ring_out,
     ring_in,
@@ -122,10 +124,15 @@
     sems = Sems(copy_sems)
 
     barrier = pltpu.get_barrier_semaphore()
-    group = [sibling] + [
-        at(x_=lax.rem(x + k, 4), core_=c_) for k in (2, 1, 3) for c_ in (core, 1 - core)
+    places = [
+        (kx, ky, kc) for kx in (2, 1, 3, 0) for ky in (2, 1, 3, 0) for kc in (0, 1)
     ]
-    partners = group + y_peer[1:] + [z_peer(1), z_peer(15)]
+    places.remove((0, 0, 0))
+    plane = [
+        at(x_=lax.rem(x + kx, 4), y_=lax.rem(y + ky, 4), core_=1 - core if kc else core)
+        for kx, ky, kc in places
+    ]
+    partners = plane + [z_peer(1), z_peer(15)]
     for partner in partners:
         pl.semaphore_signal(barrier, inc=1, device_id=partner, device_id_type=MESH)
 
@@ -143,7 +150,13 @@
         c_loads.append(load([(c_hbm.at[:, columns], c_v.at[:, columns])]))
     score_loads = [
         load([pair])
-        for pair in ((query_hbm, query_v), (ck_hbm, ck_v), (cv_hbm, cv_v), (value_hbm, value_v))
+        for pair in (
+            (query_hbm, query_v),
+            (ck_hbm, ck_v),
+            (cv_hbm, cv_v),
+            (value_hbm, value_v),
+            (lengths_hbm, lengths),
+        )
     ]
     gain_load = load([(gain_hbm, gain_v)])
     adam_load = load(
@@ -184,7 +197,7 @@
     for k in (2, 1, 3):
         remote(rows_y.at[y], rows_y.at[y], own_sent, own_sem, y_peer[k]).start()
 
-    swap_sent = sender(part.at[:, 1 - core])
+    swap_sent = sender(part_out)
     swaps = [arrival(part_in.at[j]) for j in range(CHUNKS)]
 
     def local_term(j):
@@ -199,7 +212,8 @@
         ).reshape(8, 4, 2, 16, CW)
         part[j, 0] = term[:, :, 0]
         part[j, 1] = term[:, :, 1]
-        remote(part.at[j, 1 - core], part_in.at[j], swap_sent, swaps[j][0], sibling).start()
+        part_out[j] = part[j, 1 - core].astype(BF16)
+        remote(part_out.at[j], part_in.at[j], swap_sent, swaps[j][0], sibling).start()
 
     xp, xo, xm = (lax.rem(x + k, 4) for k in (1, 2, 3))
     low, high = slice(0, 4), slice(4, 8)
@@ -216,7 +230,7 @@
     parity, quad = lax.rem(zl, 2), lax.div(zl, 2)
 
     def chip_sum(j, half, target):
-        return part[j, core, half, target] + part_in[j, half, target]
+        return part[j, core, half, target] + part_in[j, half, target].astype(F32)
 
     def ring_send(j, number, value, device):
         ring_out[j, number] = value.astype(BF16)
@@ -357,29 +371,22 @@
             old_top[rows, :] = top
             old_sum[rows, :] = jnp.sum(weight, axis=1, keepdims=True)
 
-    to_y_sent = sender(w_out.at[:, 0:3])
-    to_y = [arrival(w_out.at[h, 0:3]) for h in range(2)]
-    shared_sent = [sender(rows_z.at[0:7]) for h in range(2)]
-    shared = [arrival(rows_z.at[0:7]) for h in range(2)]
+    shared_sent = [sender(w_all.at[0, 0:31]) for h in range(2)]
+    shared = [arrival(w_all.at[0, 0:31]) for h in range(2)]
     keys_sent = sender(key_in.at[0:15, pl.ds(0, 12)])
     keys_sem, keys_here = arrival(key_in.at[0:15, pl.ds(0, 12)])
 
     def head_columns(h):
-        for k in (2, 1, 3):
+        slot = (y * 4 + x) * 2 + core
+        for (_, ky, _), device in zip(places, plane):
             remote(
-                w_out.at[h, lax.rem(y + k, 4)],
-                w_all.at[h, y, x, core],
-                to_y_sent,
-                to_y[h][0],
-                y_peer[k],
+                w_out.at[h, lax.rem(y + ky, 4)],
+                w_all.at[h, slot],
+                shared_sent[h],
+                shared[h][0],
+                device,
             ).start()
-        w_all[h, y, x, core] = w_out[h, y]
-
-    def share_weights(h):
-        to_y[h][1].wait_recv()
-        mine = w_all.at[h, :, x, core]
-        for device in group[1:] + group[:1]:
-            remote(mine, mine, shared_sent[h], shared[h][0], device).start()
+        w_all[h, slot] = w_out[h, y]
 
     def send_keys(h):
         shared[h][1].wait_recv()
@@ -443,17 +450,17 @@
         (local_term, 0),
         (hop, 1),
         (local_term, 1),
+        (ring_first, 0),
         (hop, 2),
-        (ring_first, 0),
         (local_term, 2),
+        (ring_first, 1),
         (hop, 3),
-        (ring_first, 1),
         (local_term, 3),
+        (ring_second, 0),
         (hop, 4),
-        (ring_second, 0),
         (ring_first, 2),
+        (ring_second, 1),
         (hop, 5),
-        (ring_second, 1),
         (line_pair, 0),
         (ring_first, 3),
         (hop, 6),
@@ -473,13 +480,11 @@
         (update, 1),
         (head_columns, 0),
         (update, 2),
-        (share_weights, 0),
         (update, 3),
         (head_columns, 1),
+        (old_scores,),
         (make_normed,),
         (send_keys, 0),
-        (old_scores,),
-        (share_weights, 1),
         (send_keys, 1),
         (finish,),
     )
@@ -544,7 +549,7 @@
             pltpu.VMEM((16, 128), F32),
             pltpu.VMEM((3, 4, 8, 128), F32),
         ),
-        in_specs=[hbm] * 10 + [pl.BlockSpec(memory_space=pltpu.SMEM), hbm],
+        in_specs=[hbm] * 12,
         out_specs=(vmem,) * 5,
         scratch_shapes=[
             pltpu.VMEM((1024, 1024), BF16),
@@ -556,8 +561,10 @@
             pltpu.VMEM((4, 1, 512, 128), BF16),
             pltpu.VMEM((4, 1, 512, 128), BF16),
             pltpu.VMEM((64, 128), F32),
+            pltpu.SMEM((4,), jnp.int32),
             pltpu.VMEM((CHUNKS, 2, 8, 4, 16, CW), F32),
-            pltpu.VMEM((CHUNKS, 8, 4, 16, CW), F32),
+            pltpu.VMEM((CHUNKS, 8, 4, 16, CW), BF16),
+            pltpu.VMEM((CHUNKS, 8, 4, 16, CW), BF16),
             pltpu.VMEM((CHUNKS, 6, 4, 16, CW), BF16),
             pltpu.VMEM((CHUNKS, 6, 4, 16, CW), BF16),
             pltpu.VMEM((CHUNKS, 8, 16, CW), F32),
@@ -572,7 +579,7 @@
             pltpu.VMEM((16, 1, 128), F32),
             pltpu.VMEM((128, 512), BF16),
             pltpu.VMEM((2, 4, 16, 128), BF16),
-            pltpu.VMEM((2, 4, 4, 2, 16, 128), BF16),
+            pltpu.VMEM((2, 32, 16, 128), BF16),
             pltpu.VMEM((2, 8, 16, 128), F32),
             pltpu.VMEM((16, 16, 128), F32),
             pltpu.VMEM((128, 128), F32),
@@ -601,10 +608,10 @@
                 step_values.reshape(3, 4, 128),
                 cache_keys,
                 cache_values,
+                cache_lengths,
+                norm_gain.reshape(64, 128),
             )
         ),
-        cache_lengths,
-        pltpu.with_memory_space_constraint(norm_gain.reshape(64, 128), pltpu.HBM),
     )
     new_master, new_one, new_two, new_keys, decoded = pl.pallas_call(
         store,

time: 61 us -> 58 us (0.951)
  Pallas kernels: 59.5 us -> 57.2 us
  local copies, waits for them, and re-layouts: 0.65 us -> 0.01 us
    pallas_call x1, Pallas kernels: 58.8 us -> 56.5 us  [body(): pl.pallas_call(kernel, out_shape=(owned_v, owned_v, owned_v, pltpu.VMEM((...]
    unnamed x4 -> x2, local copies, waits for them, and re-layouts: 0.65 us -> 0.01 us
where the time goes in v4:
time: 58 us; the launch traced here: 57.8 us
  Pallas kernels  57.2 us (99%)
  between operations  0.66 us (1%)
    pallas_call x1, Pallas kernels, body(): pl.pallas_call(kernel, out_shape=(owned_v, owned_v, owned_v, pltpu.VMEM((...  56.5 us

profile of v4, /device:TPU:1, one launch (start us, length us, event | category | flops | bytes accessed | tf_op | source)
XLA Modules:
  0.0 57.8 jit_solution(6231700988005983158)
XLA Ops:
  0.6 0.0 copy-start
  0.6 56.5 %adam_decode.1 = (f32[1,16,1024]{2,1,0:T(8,128)S(1)}, f32[1,16,1024]{2,1,0:T(8,128)S(1)}, f32[1,16,1024]{2,1,0:T(8,128)S(1)}, f32[16,128]{1,0:T(8,128)S(1)}, f32[3,4,8,128]{3,2,1,0:T(8,128)S(1)}) custom-call(bf16[1024,1024]{1,0:T(8,128)(2,1)} %x_hbm.1, bf16[1024,1024]{1,0:T(8,128)(2,1)} %c_hbm.1, f32[1,16,1024]{2,1,0:T(8,128)} %master_hbm.1, ...), custom_call_target="tpu_custom_call" | custom-call | tf_op jit(solution)/shard_map/adam_decode/pallas_call | solution.py:543
  57.1 0.0 copy-done
  57.1 0.7 %store_results.1 = (f32[1,16,1024]{2,1,0:T(8,128)}, f32[1,16,1024]{2,1,0:T(8,128)}, f32[1,16,1024]{2,1,0:T(8,128)}, bf16[3,4,128]{2,1,0:T(4,128)(2,1)}, bf16[3,4,1024]{2,1,0:T(4,128)(2,1)}) custom-call(f32[1,16,1024]{2,1,0:T(8,128)S(1)} %get-tuple-element.15.master_v, f32[1,16,1024]{2,1,0:T(8,128)S(1)} %get-tuple-element.16.one_v, ...), custom_call_target="tpu_custom_call" | custom-call | tf_op jit(solution)/shard_map/store_results/pallas_call | solution.py:616
Async XLA Ops:
  0.6 56.5 %copy-start = (bf16[3,4,1024]{2,1,0:T(4,128)(2,1)S(1)}, bf16[3,4,1024]{2,1,0:T(4,128)(2,1)}, u32[]{:S(2)}) copy-start(bf16[3,4,1024]{2,1,0:T(4,128)(2,1)} %step_v.1) | copy-start | bytes 73732

commit v5 on v4

--- a/solution.py
+++ b/solution.py
@@ -450,17 +450,17 @@
         (local_term, 0),
         (hop, 1),
         (local_term, 1),
+        (hop, 2),
         (ring_first, 0),
-        (hop, 2),
         (local_term, 2),
+        (hop, 3),
         (ring_first, 1),
-        (hop, 3),
         (local_term, 3),
+        (hop, 4),
         (ring_second, 0),
-        (hop, 4),
         (ring_first, 2),
+        (hop, 5),
         (ring_second, 1),
-        (hop, 5),
         (line_pair, 0),
         (ring_first, 3),
         (hop, 6),
@@ -474,15 +474,15 @@
         (line_pair, 3),
         (line_quad, 2),
         (line_quad, 3),
-        (send_rows,),
         (adam_loads,),
         (update, 0),
         (update, 1),
         (head_columns, 0),
+        (send_rows,),
+        (old_scores,),
         (update, 2),
         (update, 3),
         (head_columns, 1),
-        (old_scores,),
         (make_normed,),
         (send_keys, 0),
         (send_keys, 1),

time: 58 us -> 56 us (0.966)
  Pallas kernels: 57.2 us -> 55 us
    pallas_call x1, Pallas kernels: 56.5 us -> 54.3 us  [body(): pl.pallas_call(kernel, out_shape=(owned_v, owned_v, owned_v, pltpu.VMEM((...]
where the time goes in v5:
time: 56 us; the launch traced here: 55.6 us
  Pallas kernels  55 us (98%)
  between operations  0.66 us (1%)
    pallas_call x1, Pallas kernels, body(): pl.pallas_call(kernel, out_shape=(owned_v, owned_v, owned_v, pltpu.VMEM((...  54.3 us

profile of v5, /device:TPU:1, one launch (start us, length us, event | category | flops | bytes accessed | tf_op | source)
XLA Modules:
  0.0 55.6 jit_solution(10443552127316717155)
XLA Ops:
  0.6 0.0 copy-start
  0.6 54.3 %adam_decode.1 = (f32[1,16,1024]{2,1,0:T(8,128)S(1)}, f32[1,16,1024]{2,1,0:T(8,128)S(1)}, f32[1,16,1024]{2,1,0:T(8,128)S(1)}, f32[16,128]{1,0:T(8,128)S(1)}, f32[3,4,8,128]{3,2,1,0:T(8,128)S(1)}) custom-call(bf16[1024,1024]{1,0:T(8,128)(2,1)} %x_hbm.1, bf16[1024,1024]{1,0:T(8,128)(2,1)} %c_hbm.1, f32[1,16,1024]{2,1,0:T(8,128)} %master_hbm.1, ...), custom_call_target="tpu_custom_call" | custom-call | tf_op jit(solution)/shard_map/adam_decode/pallas_call | solution.py:543
  54.9 0.0 copy-done
  54.9 0.7 %store_results.1 = (f32[1,16,1024]{2,1,0:T(8,128)}, f32[1,16,1024]{2,1,0:T(8,128)}, f32[1,16,1024]{2,1,0:T(8,128)}, bf16[3,4,128]{2,1,0:T(4,128)(2,1)}, bf16[3,4,1024]{2,1,0:T(4,128)(2,1)}) custom-call(f32[1,16,1024]{2,1,0:T(8,128)S(1)} %get-tuple-element.15.master_v, f32[1,16,1024]{2,1,0:T(8,128)S(1)} %get-tuple-element.16.one_v, ...), custom_call_target="tpu_custom_call" | custom-call | tf_op jit(solution)/shard_map/store_results/pallas_call | solution.py:616
Async XLA Ops:
  0.6 54.3 %copy-start = (bf16[3,4,1024]{2,1,0:T(4,128)(2,1)S(1)}, bf16[3,4,1024]{2,1,0:T(4,128)(2,1)}, u32[]{:S(2)}) copy-start(bf16[3,4,1024]{2,1,0:T(4,128)(2,1)} %step_v.1) | copy-start | bytes 73732

commit v6 on v5

--- a/solution.py
+++ b/solution.py
@@ -128,6 +128,7 @@
         (kx, ky, kc) for kx in (2, 1, 3, 0) for ky in (2, 1, 3, 0) for kc in (0, 1)
     ]
     places.remove((0, 0, 0))
+    places.sort(key=lambda place: -(min(place[0], 4 - place[0]) + min(place[1], 4 - place[1])))
     plane = [
         at(x_=lax.rem(x + kx, 4), y_=lax.rem(y + ky, 4), core_=1 - core if kc else core)
         for kx, ky, kc in places
@@ -470,8 +471,8 @@
         (line_quad, 0),
         (ring_second, 3),
         (line_pair, 2),
+        (line_pair, 3),
         (line_quad, 1),
-        (line_pair, 3),
         (line_quad, 2),
         (line_quad, 3),
         (adam_loads,),

time: 56 us -> 56.1 us (level)
  no operation moved by 1% of the time
where the time goes in v6:
time: 56.1 us; the launch traced here: 55.3 us
  Pallas kernels  54.6 us (97%)
  between operations  0.66 us (1%)
    pallas_call x1, Pallas kernels, body(): pl.pallas_call(kernel, out_shape=(owned_v, owned_v, owned_v, pltpu.VMEM((...  53.9 us

profile of v6, /device:TPU:1, one launch (start us, length us, event | category | flops | bytes accessed | tf_op | source)
XLA Modules:
  0.0 55.3 jit_solution(3162364371328986368)
XLA Ops:
  0.6 0.0 copy-start
  0.6 53.9 %adam_decode.1 = (f32[1,16,1024]{2,1,0:T(8,128)S(1)}, f32[1,16,1024]{2,1,0:T(8,128)S(1)}, f32[1,16,1024]{2,1,0:T(8,128)S(1)}, f32[16,128]{1,0:T(8,128)S(1)}, f32[3,4,8,128]{3,2,1,0:T(8,128)S(1)}) custom-call(bf16[1024,1024]{1,0:T(8,128)(2,1)} %x_hbm.1, bf16[1024,1024]{1,0:T(8,128)(2,1)} %c_hbm.1, f32[1,16,1024]{2,1,0:T(8,128)} %master_hbm.1, ...), custom_call_target="tpu_custom_call" | custom-call | tf_op jit(solution)/shard_map/adam_decode/pallas_call | solution.py:544
  54.5 0.0 copy-done
  54.5 0.7 %store_results.1 = (f32[1,16,1024]{2,1,0:T(8,128)}, f32[1,16,1024]{2,1,0:T(8,128)}, f32[1,16,1024]{2,1,0:T(8,128)}, bf16[3,4,128]{2,1,0:T(4,128)(2,1)}, bf16[3,4,1024]{2,1,0:T(4,128)(2,1)}) custom-call(f32[1,16,1024]{2,1,0:T(8,128)S(1)} %get-tuple-element.15.master_v, f32[1,16,1024]{2,1,0:T(8,128)S(1)} %get-tuple-element.16.one_v, ...), custom_call_target="tpu_custom_call" | custom-call | tf_op jit(solution)/shard_map/store_results/pallas_call | solution.py:617
Async XLA Ops:
  0.6 53.9 %copy-start = (bf16[3,4,1024]{2,1,0:T(4,128)(2,1)S(1)}, bf16[3,4,1024]{2,1,0:T(4,128)(2,1)}, u32[]{:S(2)}) copy-start(bf16[3,4,1024]{2,1,0:T(4,128)(2,1)} %step_v.1) | copy-start | bytes 73732
